TPU v7x, 32 devices: a whole 2x2x4 slice. The times are simulated.
32 devices in a mesh: dp: 4 (over z), seq: 8 (over y, x, core).
Axes of the slice: x: 2, y: 2, z: 4, core: 2. Of those that a mesh axis runs over, the one named last changes fastest.
Arguments:
- queries: bfloat16 [4, 1024, 12288], P('dp', 'seq'), may hold values from -8 to 8
- keys_in: bfloat16 [4, 1024, 768], P('dp', 'seq'), may hold values from -8 to 8
- values_in: bfloat16 [4, 1024, 512], P('dp', 'seq'), may hold values from -6 to 6
- gate_cmp: float32 [4, 1024, 64], P('dp', 'seq'), may hold values from 0.05 to 0.95
- gate_win: float32 [4, 1024, 64], P('dp', 'seq'), may hold values from 0.05 to 0.95
- cotangent: bfloat16 [4, 1024, 8192], P('dp', 'seq'), may hold values from -6 to 6
- compress_key: bfloat16 [6144, 192], replicated, may hold values from -1 to 1
- compress_value: bfloat16 [4096, 128], replicated, may hold values from -0.09375 to 0.09375
Outputs:
- attended: bfloat16 [4, 1024, 8192], P('dp', 'seq')
- grad_query: bfloat16 [4, 1024, 12288], P('dp', 'seq')
- grad_key: bfloat16 [4, 1024, 768], P('dp', 'seq')
- grad_value: bfloat16 [4, 1024, 512], P('dp', 'seq')
- grad_gate_cmp: float32 [4, 1024, 64], P('dp', 'seq')
- grad_gate_win: float32 [4, 1024, 64], P('dp', 'seq')
- grad_compress_key: float32 [6144, 192], P('seq')
- grad_compress_value: float32 [4096, 128], P('seq')
All inputs are finite; a program needn't handle non-finite values.
Results may differ from a plain program's by a relative error of at most 0.023.
Values may be sent and summed in bfloat16 or wider, within the bound.
A program may use at most 192 MiB of HBM per device.

v0:
```python
import math

import jax
import jax.numpy as jnp
from jax import lax
from jax.sharding import PartitionSpec as P

BLK = 32
STRIDE = 16
WIN = 512


def from_behind(array, axis, by):
    devices = lax.axis_size(axis)
    pairs = [(i, i + by) for i in range(devices) if 0 <= i + by < devices]
    return lax.ppermute(array, axis, pairs)


def attend(query_b, keys_b, values_b, valid, gate_vals, cotangent_b):
    scaling = 1.0 / math.sqrt(query_b.shape[-1])
    scores = (
        jnp.einsum("tgcd,kgd->tgck", query_b, keys_b, preferred_element_type=jnp.float32) * scaling
    )
    scores = jnp.where(valid[:, None, None, :], scores, -1e30)
    row_max = jnp.max(scores, axis=-1, keepdims=True)
    exponent = jnp.exp(scores - row_max)
    softmax_w = exponent / jnp.sum(exponent, axis=-1, keepdims=True)
    softmax_b = softmax_w.astype(jnp.bfloat16)
    branch_out = jnp.einsum(
        "tgck,kgd->tgcd", softmax_b, values_b, preferred_element_type=jnp.float32
    )
    cotangent_f = cotangent_b.astype(jnp.float32)
    grad_gate = jnp.sum(cotangent_f * branch_out, axis=-1)
    grad_out = (gate_vals[..., None] * cotangent_f).astype(jnp.bfloat16)
    grad_v = jnp.einsum("tgck,tgcd->kgd", softmax_b, grad_out, preferred_element_type=jnp.float32)
    grad_prob = jnp.einsum("tgcd,kgd->tgck", grad_out, values_b, preferred_element_type=jnp.float32)
    row_delta = jnp.sum(grad_out.astype(jnp.float32) * branch_out, axis=-1, keepdims=True)
    grad_score = (softmax_w * (grad_prob - row_delta) * scaling).astype(jnp.bfloat16)
    grad_q = jnp.einsum("tgck,kgd->tgcd", grad_score, keys_b, preferred_element_type=jnp.float32)
    grad_k = jnp.einsum("tgck,tgcd->kgd", grad_score, query_b, preferred_element_type=jnp.float32)
    return (branch_out, grad_gate, grad_q, grad_k, grad_v)


def compress_local(extended, weight, groups):
    head_dim = weight.shape[1]
    halves = extended.reshape(-1, STRIDE, groups, head_dim)
    blocks = jnp.concatenate([halves[:-1], halves[1:]], axis=1)
    weight_cube = weight.reshape(-1, head_dim, head_dim)
    compressed = jnp.einsum(
        "bpgd,pde->bge", blocks, weight_cube, preferred_element_type=jnp.float32
    ).astype(jnp.bfloat16)
    return (blocks, compressed.reshape(blocks.shape[0], groups * head_dim))


def compress_back(blocks, weight, grad_rows, groups):
    head_dim = weight.shape[1]
    weight_cube = weight.reshape(-1, head_dim, head_dim)
    grad_round = grad_rows.reshape(-1, groups, head_dim).astype(jnp.bfloat16)
    grad_slabs = jnp.einsum(
        "bge,pde->bpgd", grad_round, weight_cube, preferred_element_type=jnp.float32
    )
    grad_weight = jnp.einsum(
        "bpgd,bge->pde", blocks, grad_round, preferred_element_type=jnp.float32
    ).reshape(-1, head_dim)
    zero_half = jnp.zeros((1, STRIDE, groups, head_dim), jnp.float32)
    grad_halves = jnp.concatenate([grad_slabs[:, :STRIDE], zero_half], axis=0) + jnp.concatenate(
        [zero_half, grad_slabs[:, STRIDE:]], axis=0
    )
    return (grad_halves.reshape(-1, groups * head_dim), grad_weight)


def on_device(
    queries, keys_in, values_in, gate_cmp, gate_win, cotangent, compress_key, compress_value
):
    rows_dev = queries.shape[1]
    kv_width = keys_in.shape[2]
    value_width = values_in.shape[2]
    head_dim = compress_key.shape[1]
    value_dim = compress_value.shape[1]
    groups = kv_width // head_dim
    heads = gate_cmp.shape[2]
    per_group = heads // groups
    shard_index = lax.axis_index("seq")
    reach_shards = (WIN + rows_dev - 1) // rows_dev
    lead_count = reach_shards * rows_dev
    own_keys = keys_in[0]
    own_values = values_in[0]
    prior_k, prior_v = ([], [])
    for distance in range(reach_shards, 0, -1):
        got_k, got_v = from_behind((own_keys, own_values), "seq", distance)
        prior_k.append(got_k)
        prior_v.append(got_v)
    lead_k = jnp.concatenate(prior_k, axis=0)
    lead_v = jnp.concatenate(prior_v, axis=0)
    window_k = jnp.concatenate([lead_k, own_keys], axis=0)
    window_v = jnp.concatenate([lead_v, own_values], axis=0)
    extended_k = jnp.concatenate(
        [lead_k[lead_count - BLK :], own_keys[: rows_dev - STRIDE]], axis=0
    )
    extended_v = jnp.concatenate(
        [lead_v[lead_count - BLK :], own_values[: rows_dev - STRIDE]], axis=0
    )
    blocks_k, comp_k = compress_local(extended_k, compress_key, groups)
    blocks_v, comp_v = compress_local(extended_v, compress_value, groups)
    all_ck, all_cv = (
        lax.all_gather(comp_k, "seq", axis=0, tiled=True),
        lax.all_gather(comp_v, "seq", axis=0, tiled=True),
    )
    block_count = all_ck.shape[0]
    cmp_keys = all_ck.reshape(block_count, groups, head_dim)
    cmp_values = all_cv.reshape(block_count, groups, value_dim)
    query_b = queries[0].reshape(rows_dev, groups, per_group, head_dim)
    cotangent_b = cotangent[0].reshape(rows_dev, groups, per_group, value_dim)
    gate_c = gate_cmp[0].reshape(rows_dev, groups, per_group)
    gate_w = gate_win[0].reshape(rows_dev, groups, per_group)
    key_count = lead_count + rows_dev
    query_pos = shard_index * rows_dev + jnp.arange(rows_dev, dtype=jnp.int32)
    key_pos = shard_index * rows_dev - lead_count + jnp.arange(key_count, dtype=jnp.int32)
    distance_grid = query_pos[:, None] - key_pos[None, :]
    window_mask = (key_pos[None, :] >= 0) & (distance_grid >= 0) & (distance_grid < WIN)
    causal_mask = (
        STRIDE * jnp.arange(block_count, dtype=jnp.int32)[None, :] <= query_pos[:, None] + 1
    )
    out_cmp, gate_grad_c, grad_q_c, grad_k_c, grad_v_c = attend(
        query_b, cmp_keys, cmp_values, causal_mask, gate_c, cotangent_b
    )
    out_win, gate_grad_w, grad_q_w, grad_k_w, grad_v_w = attend(
        query_b,
        window_k.reshape(key_count, groups, head_dim),
        window_v.reshape(key_count, groups, value_dim),
        window_mask,
        gate_w,
        cotangent_b,
    )
    attended = (
        (gate_c[..., None] * out_cmp + gate_w[..., None] * out_win)
        .astype(jnp.bfloat16)
        .reshape(rows_dev, heads * value_dim)
    )
    grad_query = (grad_q_c + grad_q_w).astype(jnp.bfloat16).reshape(rows_dev, heads * head_dim)
    own_ck, own_cv = (
        lax.psum_scatter(
            grad_k_c.reshape(block_count, kv_width).astype(jnp.bfloat16),
            "seq",
            scatter_dimension=0,
            tiled=True,
        ).astype(jnp.float32),
        lax.psum_scatter(
            grad_v_c.reshape(block_count, value_width).astype(jnp.bfloat16),
            "seq",
            scatter_dimension=0,
            tiled=True,
        ).astype(jnp.float32),
    )
    back_k, weight_k = compress_back(blocks_k, compress_key, own_ck, groups)
    back_v, weight_v = compress_back(blocks_v, compress_value, own_cv, groups)
    grad_kw = grad_k_w.reshape(key_count, kv_width)
    grad_vw = grad_v_w.reshape(key_count, value_width)
    send_k = grad_kw[:lead_count] + jnp.pad(back_k[:BLK], ((lead_count - BLK, 0), (0, 0)))
    send_v = grad_vw[:lead_count] + jnp.pad(back_v[:BLK], ((lead_count - BLK, 0), (0, 0)))
    keep_k = grad_kw[lead_count:] + jnp.pad(back_k[BLK:], ((0, STRIDE), (0, 0)))
    keep_v = grad_vw[lead_count:] + jnp.pad(back_v[BLK:], ((0, STRIDE), (0, 0)))
    for distance in range(1, reach_shards + 1):
        first_row = (reach_shards - distance) * rows_dev
        got_k, got_v = (
            from_behind(
                send_k[first_row : first_row + rows_dev].astype(jnp.bfloat16), "seq", -distance
            ).astype(jnp.float32),
            from_behind(
                send_v[first_row : first_row + rows_dev].astype(jnp.bfloat16), "seq", -distance
            ).astype(jnp.float32),
        )
        keep_k = keep_k + got_k
        keep_v = keep_v + got_v
    part_k, part_v = (
        lax.psum_scatter(
            weight_k.astype(jnp.bfloat16), "seq", scatter_dimension=0, tiled=True
        ).astype(jnp.float32),
        lax.psum_scatter(
            weight_v.astype(jnp.bfloat16), "seq", scatter_dimension=0, tiled=True
        ).astype(jnp.float32),
    )
    rows_k, rows_v = (
        lax.psum(part_k.astype(jnp.bfloat16), "dp").astype(jnp.float32),
        lax.psum(part_v.astype(jnp.bfloat16), "dp").astype(jnp.float32),
    )
    return (
        attended[None],
        grad_query[None],
        keep_k.astype(jnp.bfloat16)[None],
        keep_v.astype(jnp.bfloat16)[None],
        gate_grad_c.reshape(rows_dev, heads)[None],
        gate_grad_w.reshape(rows_dev, heads)[None],
        rows_k,
        rows_v,
    )


def solution(mesh):
    in_specs = (
        P("dp", "seq", None),
        P("dp", "seq", None),
        P("dp", "seq", None),
        P("dp", "seq", None),
        P("dp", "seq", None),
        P("dp", "seq", None),
        P(),
        P(),
    )
    out_specs = (
        P("dp", "seq", None),
        P("dp", "seq", None),
        P("dp", "seq", None),
        P("dp", "seq", None),
        P("dp", "seq", None),
        P("dp", "seq", None),
        P("seq", None),
        P("seq", None),
    )
    return jax.shard_map(
        on_device, mesh=mesh, in_specs=in_specs, out_specs=out_specs, check_vma=False
    )
```

profile of v0, /device:TPU:3, one launch (start us, length us, event | category | flops | bytes accessed | tf_op | source)
XLA Modules:
  0.0 329.9 jit_solution(13268440887416935137)
XLA Ops:
  7.2 3.3 collective-permute-start.4
  14.4 3.3 %collective-permute-start = (bf16[128,512]{1,0:T(8,128)(2,1)}, bf16[128,512]{1,0:T(8,128)(2,1)}, u32[]{:S(2)}, u32[]{:S(2)}) collective-permute-start(bf16[128,512]{1,0:T(8,128)(2,1)} %bitcast.285), channel_id=1, source_target_pairs={{0,1},{1,2},{2,3},{3,4},{4,5},{5,6},{6,7},{8,9},{9,10},{10,11},{11... | collective-permute-start | bytes 393224 | tf_op jit(solution)/shard_map/ppermute | solution.py:16
  25.6 4.8 %copy.53 = bf16[1,128,12288]{1,2,0:T(8,128)(2,1)} copy(bf16[1,128,12288]{2,1,0:T(8,128)(2,1)} %param.8) | data formatting | bytes 6291456 | tf_op args[0]
  33.1 4.3 %copy.67 = f32[1,128,8192]{1,2,0:T(8,128)} copy(bf16[1,128,8192]{2,1,0:T(8,128)(2,1)} %param.13) | data formatting | bytes 6291456 | tf_op jit(solution)/shard_map/convert_element_type | solution.py:32
  44.7 11.1 %all_gather.6 = bf16[64,512]{1,0:T(8,128)(2,1)S(1)} all-gather(bf16[8,512]{1,0:T(8,128)(2,1)S(1)} %fusion.30), channel_id=1, replica_groups=mesh['dp'=4,'seq'=8] {'seq'}, dimensions={0}, use_global_device_ids=true | all-gather | bytes 73728 | tf_op jit(solution)/shard_map/all_gather | solution.py:107
  56.5 3.2 collective-permute-start.1
  67.4 8.6 %all_gather.7 = bf16[64,768]{1,0:T(8,128)(2,1)S(1)} all-gather(bf16[8,768]{1,0:T(8,128)(2,1)S(1)} %reshape.180), channel_id=1, replica_groups=mesh['dp'=4,'seq'=8] {'seq'}, dimensions={0}, use_global_device_ids=true | all-gather | bytes 110592 | tf_op jit(solution)/shard_map/all_gather | solution.py:106
  86.2 3.6 %fusion.60 = f32[4,128,128,16]{2,1,3,0:T(8,128)} fusion(bf16[64,4,128,1]{2,1,0,3:T(4,128)(2,1)} %bitcast.290, f32[128,4,16]{0,2,1:T(8,128)} %get-tuple-element.51, f32[4,64,128,16]{2,1,3,0:T(8,128)S(1)} %fusion.57, pred[128,64]{0,1:T(8,128)(4,1)S(1)} %broadcast_compare_fusion), kind=kOutput, calls=%fused_computation.109 | convolution fusion | flops 136847424 | bytes 6397952 | tf_op jit(solution)/shard_map/tgck,kgd->tgcd/dot_general | solution.py:29
  89.8 12.5 %fusion.76 = (f32[128,4,16]{0,2,1:T(8,128)S(1)}, f32[128,4,16,640]{0,3,2,1:T(8,128)}) fusion(pred[128,640]{0,1:T(8,128)(4,1)S(1)} %copy-done.27, bf16[128,4,16,192]{0,3,2,1:T(8,128)(2,1)} %bitcast.251, bf16[640,4,192]{0,2,1:T(8,128)(2,1)} %copy-done.18), kind=kOutput, calls=%fused_computation.139 | convolution fusion | flops 2034238080 | bytes 25214976 | tf_op jit(solution)/shard_map/sub | solution.py:26
  102.3 10.4 %fusion.9 = bf16[128,4,16,640]{0,3,2,1:T(8,128)(2,1)S(1)} fusion(f32[128,4,16,640]{0,3,2,1:T(8,128)} %get-tuple-element.50, f32[128,4,16]{0,2,1:T(8,128)S(1)} %get-tuple-element.49), kind=kLoop, calls=%fused_computation.13 | loop fusion | flops 10485760 | bytes 31490048 | tf_op jit(solution)/shard_map/convert_element_type | solution.py:28
  112.8 5.8 %fusion.15 = (f32[128,4,16]{0,2,1:T(8,128)}, f32[128,4,16]{0,2,1:T(8,128)}, f32[128,4,16]{0,2,1:T(8,128)}, f32[128,4,16]{0,2,1:T(8,128)}, bf16[128,4,16,128]{0,3...) fusion(f32[128,4,16,128]{0,3,2,1:T(8,128)S(1)} %bitcast.256, ...), kind=kOutput, calls=%fused_computation.25 | convolution fusion | flops 1361018880 | bytes 26017792 | tf_op jit(solution)/shard_map/tgck,kgd->tgcd/dot_general | solution.py:29
  118.6 3.2 fusion.27
  122.8 3.1 fusion.20
  125.9 12.3 %fusion.4 = bf16[128,4,16,640]{0,3,2,1:T(8,128)(2,1)} fusion(f32[128,4,16]{0,2,1:T(8,128)S(1)} %copy-done.33, f32[128,4,16,640]{0,3,2,1:T(8,128)} %get-tuple-element.50, f32[128,4,16]{0,2,1:T(8,128)S(1)} %copy-done.32, bf16[128,4,16,128]{0,3,2,1:T(8,128)(2,1)S(1)} %copy-done.6, bf16[640,4,128]{0,2,1:T(8,128)(2,1)} %copy-done.21), kind=kOutput, calls=%fused_computation.5 | convolution fusion | flops 1368391680 | bytes 34275328 | tf_op jit(solution)/shard_map/tgcd,kgd->tgck/dot_general | solution.py:36
  140.2 16.3 %reduce-scatter.7.cloned.1.call-done = bf16[8,512]{1,0:T(8,128)(2,1)} async-done(((bf16[64,512]{1,0:T(8,128)(2,1)}), bf16[8,512]{1,0:T(8,128)(2,1)}) %reduce-scatter.7.cloned.1.call-update) | async-done | bytes 8208 | tf_op jit(solution)/shard_map/reduce_scatter | solution.py:148
  158.9 8.0 %convolution_bitcast_fusion.3 = f32[640,4,128]{0,2,1:T(8,128)S(1)} fusion(bf16[128,4,16,128]{0,3,2,1:T(8,128)(2,1)} %get-tuple-element.31, bf16[128,4,16,640]{0,3,2,1:T(8,128)(2,1)} %copy-done.1), kind=kOutput, calls=%fused_computation.43 | convolution fusion | flops 1342177280 | bytes 13893632 | tf_op jit(solution)/shard_map/tgck,tgcd->kgd/dot_general | solution.py:35
  168.8 8.9 %convolution_bitcast_fusion.2 = f32[640,4,192]{0,2,1:T(8,128)} fusion(bf16[128,4,16,640]{0,3,2,1:T(8,128)(2,1)} %fusion.4, bf16[128,4,16,192]{0,3,2,1:T(8,128)(2,1)S(1)} %bitcast.253), kind=kOutput, calls=%fused_computation.41 | convolution fusion | flops 2013265920 | bytes 15597568 | tf_op jit(solution)/shard_map/tgck,tgcd->kgd/dot_general | solution.py:40
  183.0 9.8 %reduce-scatter.5.cloned.1.call-done = bf16[8,768]{1,0:T(8,128)(2,1)} async-done(((bf16[64,768]{1,0:T(8,128)(2,1)}), bf16[8,768]{1,0:T(8,128)(2,1)}) %reduce-scatter.5.cloned.1.call-update) | async-done | bytes 12304 | tf_op jit(solution)/shard_map/reduce_scatter | solution.py:142
  196.2 5.8 %fusion.37 = f32[4,192,128,16]{2,1,3,0:T(8,128)S(1)} fusion(bf16[128,4,16,640]{0,3,2,1:T(8,128)(2,1)} %fusion.4, bf16[640,4,192]{0,2,1:T(8,128)(2,1)} %copy-done.18), kind=kOutput, calls=%fused_computation.65 | convolution fusion | flops 2013265920 | bytes 17760256 | tf_op jit(solution)/shard_map/tgck,kgd->tgcd/dot_general | solution.py:39
  204.7 4.7 %copy.92 = bf16[1,128,12288]{2,1,0:T(8,128)(2,1)} copy(bf16[1,128,12288]{1,2,0:T(8,128)(2,1)} %bitcast.257) | data formatting | bytes 6291456
  213.8 3.1 copy.81
  240.7 40.9 %reduce-scatter.9.cloned.1.call-done = bf16[768,192]{0,1:T(8,128)(2,1)} async-done(((bf16[6144,192]{0,1:T(8,128)(2,1)}), bf16[768,192]{0,1:T(8,128)(2,1)}) %reduce-scatter.9.cloned.1.call-update) | async-done | bytes 294928 | tf_op jit(solution)/shard_map/reduce_scatter | solution.py:176
  289.8 5.9 %collective-permute-done.11 = bf16[128,768]{1,0:T(8,128)(2,1)S(1)} collective-permute-done((bf16[128,768]{1,0:T(8,128)(2,1)S(1)}, bf16[128,768]{1,0:T(8,128)(2,1)S(1)}, u32[]{:S(2)}, u32[]{:S(2)}) %collective-permute-start.11) | collective-permute-done | bytes 196640 | tf_op jit(solution)/shard_map/ppermute | solution.py:16
  299.4 20.5 %all-reduce.11.cloned.1.call-done = (bf16[768,192]{0,1:T(8,128)(2,1)}, bf16[512,128]{1,0:T(8,128)(2,1)}) async-done(((bf16[768,192]{0,1:T(8,128)(2,1)}, bf16[512,128]{1,0:T(8,128)(2,1)}), (bf16[768,192]{0,1:T(8,128)(2,1)}, bf16[512,128]{1,0:T(8,128)(2,1)})) %all-reduce.11.cloned.1.call-update) | async-done | bytes 426000 | tf_op jit(solution)/shard_map/psum | solution.py:184
  (202 shorter events, 102.0 us)
Async XLA Ops:
  7.2 34.3 %copy-start = (bf16[4096,128]{1,0:T(8,128)(2,1)S(1)}, bf16[4096,128]{1,0:T(8,128)(2,1)}, u32[]{:S(2)}) copy-start(bf16[4096,128]{1,0:T(8,128)(2,1)} %param.15) | copy-start | bytes 3145732
  7.2 149.3 %reduce-scatter.7.cloned.1.call-start = ((), (), s32[]{:S(2)}) async-start(), calls=%async_computation.5 | async-start | bytes 73728 | tf_op jit(solution)/shard_map/reduce_scatter | solution.py:148
  7.2 53.5 %collective-permute-start.4 = (bf16[128,512]{1,0:T(8,128)(2,1)}, bf16[128,512]{1,0:T(8,128)(2,1)}, u32[]{:S(2)}, u32[]{:S(2)}) collective-permute-start(bf16[128,512]{1,0:T(8,128)(2,1)} %bitcast.282), channel_id=1, source_target_pairs={{0,2},{1,3},{2,4},{3,5},{4,6},{5,7},{8,10},{9,11},{10,12},{11,13},... | collective-permute-start | bytes 393224 | tf_op jit(solution)/shard_map/ppermute | solution.py:16
  10.5 46.0 %collective-permute-start.3 = (bf16[128,512]{1,0:T(8,128)(2,1)}, bf16[128,512]{1,0:T(8,128)(2,1)}, u32[]{:S(2)}, u32[]{:S(2)}) collective-permute-start(bf16[128,512]{1,0:T(8,128)(2,1)} %bitcast.283), channel_id=1, source_target_pairs={{0,3},{1,4},{2,5},{3,6},{4,7},{8,11},{9,12},{10,13},{11,14},{12,15... | collective-permute-start | bytes 393224 | tf_op jit(solution)/shard_map/ppermute | solution.py:16
  12.4 29.3 %collective-permute-start.2 = (bf16[128,512]{1,0:T(8,128)(2,1)}, bf16[128,512]{1,0:T(8,128)(2,1)}, u32[]{:S(2)}, u32[]{:S(2)}) collective-permute-start(bf16[128,512]{1,0:T(8,128)(2,1)} %bitcast.284), channel_id=1, source_target_pairs={{0,4},{1,5},{2,6},{3,7},{8,12},{9,13},{10,14},{11,15},{16,20},{17,... | collective-permute-start | bytes 393224 | tf_op jit(solution)/shard_map/ppermute | solution.py:16
  14.4 24.0 %collective-permute-start = (bf16[128,512]{1,0:T(8,128)(2,1)}, bf16[128,512]{1,0:T(8,128)(2,1)}, u32[]{:S(2)}, u32[]{:S(2)}) collective-permute-start(bf16[128,512]{1,0:T(8,128)(2,1)} %bitcast.285), channel_id=1, source_target_pairs={{0,1},{1,2},{2,3},{3,4},{4,5},{5,6},{6,7},{8,9},{9,10},{10,11},{11... | collective-permute-start | bytes 393224 | tf_op jit(solution)/shard_map/ppermute | solution.py:16
  17.7 60.9 %collective-permute-start.7 = (bf16[128,768]{1,0:T(8,128)(2,1)}, bf16[128,768]{1,0:T(8,128)(2,1)}, u32[]{:S(2)}, u32[]{:S(2)}) collective-permute-start(bf16[128,768]{1,0:T(8,128)(2,1)} %bitcast.273), channel_id=1, source_target_pairs={{0,2},{1,3},{2,4},{3,5},{4,6},{5,7},{8,10},{9,11},{10,12},{11,13},... | collective-permute-start | bytes 589832 | tf_op jit(solution)/shard_map/ppermute | solution.py:16
  37.5 25.5 %copy-start.25 = (bf16[112,768]{1,0:T(8,128)(2,1)S(1)}, bf16[112,768]{1,0:T(8,128)(2,1)}, u32[]{:S(2)}) copy-start(bf16[112,768]{1,0:T(8,128)(2,1)} %slice_bitcast_fusion) | copy-start | bytes 516100
  38.4 37.8 %collective-permute-start.6 = (bf16[128,768]{1,0:T(8,128)(2,1)S(1)}, bf16[128,768]{1,0:T(8,128)(2,1)}, u32[]{:S(2)}, u32[]{:S(2)}) collective-permute-start(bf16[128,768]{1,0:T(8,128)(2,1)S(1)} %bitcast.274), channel_id=1, source_target_pairs={{0,3},{1,4},{2,5},{3,6},{4,7},{8,11},{9,12},{10,13},{11,14},{12,15... | collective-permute-start | bytes 589832 | tf_op jit(solution)/shard_map/ppermute | solution.py:16
  41.7 35.6 %collective-permute-start.5 = (bf16[128,768]{1,0:T(8,128)(2,1)S(1)}, bf16[128,768]{1,0:T(8,128)(2,1)}, u32[]{:S(2)}, u32[]{:S(2)}) collective-permute-start(bf16[128,768]{1,0:T(8,128)(2,1)S(1)} %bitcast.275), channel_id=1, source_target_pairs={{0,4},{1,5},{2,6},{3,7},{8,12},{9,13},{10,14},{11,15},{16,20},{17,... | collective-permute-start | bytes 589832 | tf_op jit(solution)/shard_map/ppermute | solution.py:16
  56.5 6.4 %collective-permute-start.1 = (bf16[128,768]{1,0:T(8,128)(2,1)S(1)}, bf16[128,768]{1,0:T(8,128)(2,1)S(1)}, u32[]{:S(2)}, u32[]{:S(2)}) collective-permute-start(bf16[128,768]{1,0:T(8,128)(2,1)S(1)} %bitcast.276), channel_id=1, source_target_pairs={{0,1},{1,2},{2,3},{3,4},{4,5},{5,6},{6,7},{8,9},{9,10},{10,11},{11... | collective-permute-start | bytes 589832 | tf_op jit(solution)/shard_map/ppermute | solution.py:16
  122.5 70.3 %reduce-scatter.5.cloned.1.call-start = ((), (), s32[]{:S(2)}) async-start(), calls=%async_computation.4 | async-start | bytes 110592 | tf_op jit(solution)/shard_map/reduce_scatter | solution.py:142
  140.2 100.5 %reduce-scatter.11.cloned.1.call-start = ((), (), s32[]{:S(2)}) async-start(), calls=%async_computation.7 | async-start | bytes 1179648 | tf_op jit(solution)/shard_map/reduce_scatter | solution.py:179
  158.8 122.8 %reduce-scatter.9.cloned.1.call-start = ((), (), s32[]{:S(2)}) async-start(), calls=%async_computation.6 | async-start | bytes 2654208 | tf_op jit(solution)/shard_map/reduce_scatter | solution.py:176
  195.9 124.0 %all-reduce.11.cloned.1.call-start = ((), (), s32[]{:S(2)}) async-start(), calls=%async_computation.8 | async-start | bytes 851968 | tf_op jit(solution)/shard_map/psum | solution.py:184
  223.1 58.6 %collective-permute-start.12 = (bf16[128,512]{1,0:T(8,128)(2,1)}, bf16[128,512]{1,0:T(8,128)(2,1)}, u32[]{:S(2)}, u32[]{:S(2)}) collective-permute-start(bf16[128,512]{1,0:T(8,128)(2,1)} %get-tuple-element.39), channel_id=1, source_target_pairs={{1,0},{2,1},{3,2},{4,3},{5,4},{6,5},{7,6},{9,8},{10,9},{11,10},{12... | collective-permute-start | bytes 393224 | tf_op jit(solution)/shard_map/ppermute | solution.py:16
  226.1 56.9 %collective-permute-start.15 = (bf16[128,512]{1,0:T(8,128)(2,1)}, bf16[128,512]{1,0:T(8,128)(2,1)}, u32[]{:S(2)}, u32[]{:S(2)}) collective-permute-start(bf16[128,512]{1,0:T(8,128)(2,1)} %get-tuple-element.40), channel_id=1, source_target_pairs={{4,0},{5,1},{6,2},{7,3},{12,8},{13,9},{14,10},{15,11},{20,16},{21,... | collective-permute-start | bytes 393224 | tf_op jit(solution)/shard_map/ppermute | solution.py:16
  227.4 58.4 %collective-permute-start.14 = (bf16[128,512]{1,0:T(8,128)(2,1)}, bf16[128,512]{1,0:T(8,128)(2,1)}, u32[]{:S(2)}, u32[]{:S(2)}) collective-permute-start(bf16[128,512]{1,0:T(8,128)(2,1)} %get-tuple-element.41), channel_id=1, source_target_pairs={{3,0},{4,1},{5,2},{6,3},{7,4},{11,8},{12,9},{13,10},{14,11},{15,12... | collective-permute-start | bytes 393224 | tf_op jit(solution)/shard_map/ppermute | solution.py:16
  229.3 58.4 %collective-permute-start.13 = (bf16[128,512]{1,0:T(8,128)(2,1)}, bf16[128,512]{1,0:T(8,128)(2,1)}, u32[]{:S(2)}, u32[]{:S(2)}) collective-permute-start(bf16[128,512]{1,0:T(8,128)(2,1)} %get-tuple-element.42), channel_id=1, source_target_pairs={{2,0},{3,1},{4,2},{5,3},{6,4},{7,5},{10,8},{11,9},{12,10},{13,11},... | collective-permute-start | bytes 393224 | tf_op jit(solution)/shard_map/ppermute | solution.py:16
  236.9 61.8 %copy-start.17 = (f32[128,768]{1,0:T(8,128)S(1)}, f32[128,768]{1,0:T(8,128)}, u32[]{:S(2)}) copy-start(f32[128,768]{1,0:T(8,128)} %copy.79) | copy-start | bytes 1179652
  238.8 51.0 %collective-permute-start.8 = (bf16[128,768]{1,0:T(8,128)(2,1)S(1)}, bf16[128,768]{1,0:T(8,128)(2,1)S(1)}, u32[]{:S(2)}, u32[]{:S(2)}) collective-permute-start(bf16[128,768]{1,0:T(8,128)(2,1)S(1)} %get-tuple-element.35), channel_id=1, source_target_pairs={{1,0},{2,1},{3,2},{4,3},{5,4},{6,5},{7,6},{9,8},{10,9},{11,10},{12... | collective-permute-start | bytes 589832 | tf_op jit(solution)/shard_map/ppermute | solution.py:16
  281.7 14.0 %collective-permute-start.11 = (bf16[128,768]{1,0:T(8,128)(2,1)S(1)}, bf16[128,768]{1,0:T(8,128)(2,1)S(1)}, u32[]{:S(2)}, u32[]{:S(2)}) collective-permute-start(bf16[128,768]{1,0:T(8,128)(2,1)S(1)} %get-tuple-element.36), channel_id=1, source_target_pairs={{4,0},{5,1},{6,2},{7,3},{12,8},{13,9},{14,10},{15,11},{20,16},{21,... | collective-permute-start | bytes 589832 | tf_op jit(solution)/shard_map/ppermute | solution.py:16
  283.0 15.6 %collective-permute-start.10 = (bf16[128,768]{1,0:T(8,128)(2,1)S(1)}, bf16[128,768]{1,0:T(8,128)(2,1)S(1)}, u32[]{:S(2)}, u32[]{:S(2)}) collective-permute-start(bf16[128,768]{1,0:T(8,128)(2,1)S(1)} %get-tuple-element.37), channel_id=1, source_target_pairs={{3,0},{4,1},{5,2},{6,3},{7,4},{11,8},{12,9},{13,10},{14,11},{15,12... | collective-permute-start | bytes 589832 | tf_op jit(solution)/shard_map/ppermute | solution.py:16
  285.8 12.8 %collective-permute-start.9 = (bf16[128,768]{1,0:T(8,128)(2,1)S(1)}, bf16[128,768]{1,0:T(8,128)(2,1)S(1)}, u32[]{:S(2)}, u32[]{:S(2)}) collective-permute-start(bf16[128,768]{1,0:T(8,128)(2,1)S(1)} %get-tuple-element.38), channel_id=1, source_target_pairs={{2,0},{3,1},{4,2},{5,3},{6,4},{7,5},{10,8},{11,9},{12,10},{13,11},... | collective-permute-start | bytes 589832 | tf_op jit(solution)/shard_map/ppermute | solution.py:16
  (33 other events, 229.8 us)
Sparse Core Ops, SparseCore 0:
  122.6 33.8 reduce-scatter.6
  160.4 32.3 reduce-scatter.4
  196.3 39.4 reduce-scatter.10
  239.4 42.1 reduce-scatter.8
  283.9 35.9 all-reduce.10
where the time goes:
time: 334 us; the launch traced here: 330 us
  waiting for transfers between devices  96.5 us (29%)
  matrix products  78.4 us (23%)
  local copies, waits for them, and re-layouts  61.7 us (18%)
  starting transfers between devices  36.2 us (11%)
  other arithmetic  22.7 us (7%)
  blocking collectives  19.7 us (6%)
  between operations  14.7 us (4%)
    reduce_scatter x1, waiting for transfers between devices, on_device(): lax.psum_scatter(weight_k.astype(jnp.bfloat16), 'seq', scatter_dimension=...  40.9 us
    ppermute x16, starting transfers between devices, from_behind(): return lax.ppermute(array, axis, pairs)  35.5 us
    psum x1, waiting for transfers between devices, on_device(): lax.psum(part_k.astype(jnp.bfloat16), 'dp').astype(jnp.float32)  20.5 us
    unnamed x87, local copies, waits for them, and re-layouts  19.7 us
    reduce_scatter x1, waiting for transfers between devices, on_device(): lax.psum_scatter(grad_v_c.reshape(block_count, value_width).astype(jnp.bf...  16.3 us
    dot_general x2, matrix products, attend(): jnp.einsum('tgcd,kgd->tgck', grad_out, values_b, preferred_element_type=j...  15.3 us
    sub x1, matrix products, attend(): exponent = jnp.exp(scores - row_max)  12.5 us
    dot_general x2, matrix products, attend(): jnp.einsum('tgck,tgcd->kgd', softmax_b, grad_out, preferred_element_type=...  11.2 us
  transfers between devices with their start and end apart: 21, of which 6 were waited for; matrix products, arithmetic and copies ran while one was open for 35% of the time, Pallas kernels for 0%

commit v1 on v0

v1 whole, which is shorter than its diff:
```python
import functools
import math

import jax
import jax.numpy as jnp
from jax import lax
from jax.experimental import pallas as pl
from jax.experimental.pallas import tpu as pltpu
from jax.sharding import PartitionSpec as P

BLK = 32
STRIDE = 16
WIN = 512
NEG = -1e30
F32 = jnp.float32
BF16 = jnp.bfloat16
VLIM = 56 * 1024 * 1024


def mm(a, b, ca, cb):
    return lax.dot_general(a, b, (((ca,), (cb,)), ((), ())), preferred_element_type=F32)


def full(memory=pltpu.VMEM):
    return pl.BlockSpec(memory_space=memory)


def up128(n):
    return (n + 127) // 128 * 128


def stack_groups(rows, groups, width):
    return jnp.concatenate([rows[:, g * width : (g + 1) * width] for g in range(groups)], axis=0)


def fill_padded(pad_ref, kv_ref):
    for i in range(pad_ref.shape[0]):
        pad_ref[i, 0:BLK, :] = jnp.zeros((BLK, 128), F32)
        pad_ref[i, BLK:, :] = kv_ref[:, 128 * i : 128 * (i + 1)].astype(F32)


def every_stride(pad_ref, p, nb):
    tiles = [pad_ref[i, pl.ds(p, nb, stride=STRIDE), :] for i in range(pad_ref.shape[0])]
    return jnp.concatenate(tiles, axis=1)


def prep_kernel(dims, kv_ref, wk_ref, wv_ref, k_ref, kt_ref, v_ref, vt_ref, pad_ref):
    groups, dk, dv, rows, reach, nb = dims
    kw = groups * dk
    index = lax.axis_index("seq")
    win = (reach + 1) * rows
    fill_padded(pad_ref, kv_ref)
    for c in range(reach + 1):
        shard = jnp.maximum(index - reach + c, 0)
        chunk = kv_ref[pl.ds(pl.multiple_of(shard * rows, rows), rows), :]
        for g in range(groups):
            k_ref[g, c * rows : (c + 1) * rows, :] = chunk[:, g * dk : (g + 1) * dk]
            v_ref[g, c * rows : (c + 1) * rows, :] = chunk[:, kw + g * dv : kw + (g + 1) * dv]
    ck = jnp.zeros((groups * nb, dk), F32)
    cv = jnp.zeros((groups * nb, dv), F32)
    for p in range(BLK):
        at = every_stride(pad_ref, p, nb).astype(BF16)
        ck += mm(stack_groups(at[:, :kw], groups, dk), wk_ref[p * dk : (p + 1) * dk, :], 1, 0)
        cv += mm(stack_groups(at[:, kw:], groups, dv), wv_ref[p * dv : (p + 1) * dv, :], 1, 0)
    for g in range(groups):
        k_ref[g, win:, :] = ck[g * nb : (g + 1) * nb].astype(BF16)
        v_ref[g, win:, :] = cv[g * nb : (g + 1) * nb].astype(BF16)
        kt_ref[g] = k_ref[g].T
        vt_ref[g] = v_ref[g].T


def prep(kv_all, wk, wv, groups, rows, reach):
    dk, dv = wk.shape[1], wv.shape[1]
    nb = kv_all.shape[0] // STRIDE
    total = (reach + 1) * rows + nb
    dims = (groups, dk, dv, rows, reach, nb)
    sds = lambda *s: jax.ShapeDtypeStruct(s, BF16)
    return pl.pallas_call(
        functools.partial(prep_kernel, dims),
        out_shape=(
            sds(groups, total, dk),
            sds(groups, dk, total),
            sds(groups, total, dv),
            sds(groups, dv, total),
        ),
        in_specs=[full()] * 3,
        out_specs=(full(),) * 4,
        scratch_shapes=[pltpu.VMEM((kv_all.shape[1] // 128, kv_all.shape[0] + BLK, 128), F32)],
        compiler_params=pltpu.CompilerParams(vmem_limit_bytes=VLIM),
    )(kv_all, wk, wv)


def back_kernel(dims, gc_ref, kv_ref, wk_ref, wv_ref, gwk_ref, gwv_ref, own_ref, pad_ref, gf_ref, own_s):
    groups, dk, dv, rows, nb, off = dims
    kw = groups * dk
    index = lax.axis_index("seq")
    per = gwk_ref.shape[0] // dk
    blocks = rows // STRIDE
    fill_padded(pad_ref, kv_ref)
    gk = gc_ref[:, :dk]
    gv = gc_ref[:, off : off + dv]
    for i in range(per):
        at = every_stride(pad_ref, index * per + i, nb)
        kst = stack_groups(at[:, :kw], groups, dk).T.astype(BF16)
        vst = stack_groups(at[:, kw:], groups, dv).T.astype(BF16)
        gwk_ref[i * dk : (i + 1) * dk, :] = mm(kst, gk, 1, 0).astype(BF16)
        gwv_ref[i * dv : (i + 1) * dv, :] = mm(vst, gv, 1, 0).astype(BF16)
    for g in range(groups):
        gf_ref[g, 0:nb, :] = gc_ref[g * nb : (g + 1) * nb, :].astype(F32)
        gf_ref[g, nb:, :] = jnp.zeros((gf_ref.shape[1] - nb, gf_ref.shape[2]), F32)
    base = pl.multiple_of(index * blocks, blocks)
    ahead = [gf_ref[g, pl.ds(base, blocks + 8), :] for g in range(groups)]
    near = jnp.concatenate([x[1 : blocks + 1] for x in ahead], axis=0)
    far = jnp.concatenate([x[2 : blocks + 2] for x in ahead], axis=0)
    near, far = near.astype(BF16), far.astype(BF16)
    for q in range(STRIDE):
        lo, hi = q, q + STRIDE
        k = mm(far[:, :dk], wk_ref[lo * dk : (lo + 1) * dk, :], 1, 1)
        k += mm(near[:, :dk], wk_ref[hi * dk : (hi + 1) * dk, :], 1, 1)
        v = mm(far[:, off : off + dv], wv_ref[lo * dv : (lo + 1) * dv, :], 1, 1)
        v += mm(near[:, off : off + dv], wv_ref[hi * dv : (hi + 1) * dv, :], 1, 1)
        parts = [k[g * blocks : (g + 1) * blocks] for g in range(groups)]
        parts += [v[g * blocks : (g + 1) * blocks] for g in range(groups)]
        row = jnp.concatenate(parts, axis=1)
        for i in range(own_s.shape[0]):
            own_s[i, pl.ds(q, blocks, stride=STRIDE), :] = row[:, 128 * i : 128 * (i + 1)]
    for i in range(own_s.shape[0]):
        own_ref[:, 128 * i : 128 * (i + 1)] = own_s[i]


def back(gc, kv_all, wk, wv, groups, rows, off, devices):
    dk, dv = wk.shape[1], wv.shape[1]
    nb = kv_all.shape[0] // STRIDE
    dims = (groups, dk, dv, rows, nb, off)
    return pl.pallas_call(
        functools.partial(back_kernel, dims),
        out_shape=(
            jax.ShapeDtypeStruct((wk.shape[0] // devices, dk), BF16),
            jax.ShapeDtypeStruct((wv.shape[0] // devices, dv), BF16),
            jax.ShapeDtypeStruct((rows, kv_all.shape[1]), F32),
        ),
        in_specs=[full()] * 4,
        out_specs=(full(),) * 3,
        scratch_shapes=[
            pltpu.VMEM((kv_all.shape[1] // 128, kv_all.shape[0] + BLK, 128), F32),
            pltpu.VMEM((groups, nb + 8, gc.shape[1]), F32),
            pltpu.VMEM((kv_all.shape[1] // 128, rows, 128), F32),
        ],
        compiler_params=pltpu.CompilerParams(vmem_limit_bytes=VLIM),
    )(gc, kv_all, wk, wv)


def bias_win(index, rows, reach):
    count = (reach + 1) * rows
    j = lax.broadcasted_iota(jnp.int32, (count, 2 * rows), 0) - reach * rows
    t = lax.broadcasted_iota(jnp.int32, (count, 2 * rows), 1)
    t = jnp.where(t >= rows, t - rows, t)
    ok = (j <= t) & (t - j < WIN) & (j + index * rows >= 0)
    return jnp.where(ok, 0.0, NEG).astype(F32)


def bias_cmp(index, rows, nb):
    b = lax.broadcasted_iota(jnp.int32, (nb, 2 * rows), 0)
    t = lax.broadcasted_iota(jnp.int32, (nb, 2 * rows), 1)
    t = jnp.where(t >= rows, t - rows, t)
    return jnp.where(STRIDE * b <= t + index * rows + 1, 0.0, NEG).astype(F32)


def branch(s, cp, bias, gate, scaling):
    s = s * (scaling * math.log2(math.e)) + bias
    e = jnp.exp2(s - jnp.max(s, axis=0, keepdims=True))
    inv = 1.0 / jnp.sum(e, axis=0, keepdims=True)
    gg = jnp.sum(e * cp, axis=0, keepdims=True) * inv
    w = (e * (gate * inv)).astype(BF16)
    gs = (e * (cp - gg) * (gate * (inv * scaling))).astype(BF16)
    return gg, w, gs


def load_pair(i, rows, dk, dv, q_ref, c_ref, qs, cs):
    base = 2 * i * rows
    both = q_ref[:, 2 * i * dk : 2 * (i + 1) * dk]
    qs[base : base + rows, :] = both[:, :dk]
    qs[base + rows : base + 2 * rows, :] = both[:, dk:]
    cs[base : base + rows, :] = c_ref[:, 2 * i * dv : (2 * i + 1) * dv]
    cs[base + rows : base + 2 * rows, :] = c_ref[:, (2 * i + 1) * dv : (2 * i + 2) * dv]
    return qs[base : base + 2 * rows, :], cs[base : base + 2 * rows, :]


def pair_gate(gate_t, first, i):
    return jnp.concatenate([gate_t[2 * i : 2 * i + 1, :], gate_t[2 * i + 1 : 2 * i + 2, :]], axis=1)


def cmp_kernel(dims, q_ref, c_ref, k_ref, v_ref, gate_ref, out_ref, bias, gate_s, qs, cs, ws, gss):
    rows, per, dk, dv, nb, off, reach = dims
    win = (reach + 1) * rows
    step = pl.program_id(0)

    @pl.when(step == 0)
    def _():
        bias[...] = bias_cmp(lax.axis_index("seq"), rows, nb)
        gate_s[...] = gate_ref[...].T

    gate_t = gate_s[pl.ds(pl.multiple_of(step * per, per), per), :]
    k = k_ref[0, win:, :]
    v = v_ref[0, win:, :]
    scaling = 1.0 / math.sqrt(dk)
    for i in range(per // 2):
        q2, c2 = load_pair(i, rows, dk, dv, q_ref, c_ref, qs, cs)
        gate = pair_gate(gate_t, 0, i)
        _, w, gs = branch(mm(k, q2, 1, 1), mm(v, c2, 1, 1), bias[...], gate, scaling)
        ws[:, 2 * i * rows : 2 * (i + 1) * rows] = w
        gss[:, 2 * i * rows : 2 * (i + 1) * rows] = gs
    out_ref[:, :dk] = mm(gss[...], qs[...], 1, 0).astype(BF16)
    if off > dk:
        out_ref[:, dk:off] = jnp.zeros((nb, off - dk), BF16)
    out_ref[:, off:] = mm(ws[...], cs[...], 1, 0).astype(BF16)


def cmp_grads(q, c, kall, vall, gate, groups, reach, nb, off):
    rows = q.shape[0]
    heads = gate.shape[1]
    per = heads // groups
    dk, dv, total = kall.shape[2], vall.shape[2], kall.shape[1]
    dims = (rows, per, dk, dv, nb, off, reach)
    return pl.pallas_call(
        functools.partial(cmp_kernel, dims),
        grid=(groups,),
        out_shape=jax.ShapeDtypeStruct((groups * nb, off + dv), BF16),
        in_specs=[
            pl.BlockSpec((rows, per * dk), lambda g: (0, g)),
            pl.BlockSpec((rows, per * dv), lambda g: (0, g)),
            pl.BlockSpec((1, total, dk), lambda g: (g, 0, 0)),
            pl.BlockSpec((1, total, dv), lambda g: (g, 0, 0)),
            pl.BlockSpec((rows, heads), lambda g: (0, 0)),
        ],
        out_specs=pl.BlockSpec((nb, off + dv), lambda g: (g, 0)),
        scratch_shapes=[
            pltpu.VMEM((nb, 2 * rows), F32),
            pltpu.VMEM((heads, rows), F32),
            pltpu.VMEM((per * rows, dk), BF16),
            pltpu.VMEM((per * rows, dv), BF16),
            pltpu.VMEM((nb, per * rows), BF16),
            pltpu.VMEM((nb, per * rows), BF16),
        ],
        compiler_params=pltpu.CompilerParams(vmem_limit_bytes=VLIM),
    )(q, c, kall, vall, gate)


def main_kernel(dims, alias, *refs):
    rows, hc, chunks, dk, dv, nb, off, reach, first = dims
    q_ref, c_ref, k_ref, kt_ref, v_ref, vt_ref, gc_ref, gw_ref = refs[:8]
    refs = refs[10:] if alias else refs[8:]
    att_ref, gq_ref, send_ref, own_ref, ggc_ref, ggw_ref = refs[:6]
    bias, gct, gwt, ggct, ggwt, qs, cs, ws, gss, acck, accv = refs[6:]
    win = (reach + 1) * rows
    lead = reach * rows
    g, part = pl.program_id(0), pl.program_id(1)
    step = g * chunks + part

    @pl.when(step == 0)
    def _():
        index = lax.axis_index("seq")
        bias[:win, :] = bias_win(index, rows, reach)
        bias[win:, :] = bias_cmp(index, rows, nb)
        gct[...] = gc_ref[...].T
        gwt[...] = gw_ref[...].T

    row0 = pl.multiple_of(step * hc, hc)
    head0 = pl.multiple_of(first * hc * chunks + step * hc, hc)
    gate_c = gct[pl.ds(head0, hc), :]
    gate_w = gwt[pl.ds(head0, hc), :]
    scaling = 1.0 / math.sqrt(dk)
    rows_c, rows_w = [], []
    for i in range(hc // 2):
        q2, c2 = load_pair(i, rows, dk, dv, q_ref, c_ref, qs, cs)
        s = mm(k_ref[0], q2, 1, 1)
        cp = mm(v_ref[0], c2, 1, 1)
        gg_w, w_w, gs_w = branch(s[:win], cp[:win], bias[:win, :], pair_gate(gate_w, 0, i), scaling)
        gg_c, w_c, gs_c = branch(s[win:], cp[win:], bias[win:, :], pair_gate(gate_c, 0, i), scaling)
        cols = slice(2 * i * rows, 2 * (i + 1) * rows)
        ws[:win, cols] = w_w
        ws[win:, cols] = w_c
        gss[:win, cols] = gs_w
        gss[win:, cols] = gs_c
        rows_w += [gg_w[:, :rows], gg_w[:, rows:]]
        rows_c += [gg_c[:, :rows], gg_c[:, rows:]]
        att = mm(vt_ref[0], ws[:, cols], 1, 0)
        gq = mm(kt_ref[0], gss[:, cols], 1, 0)
        att = jnp.concatenate([att[:, :rows], att[:, rows:]], axis=0)
        gq = jnp.concatenate([gq[:, :rows], gq[:, rows:]], axis=0)
        att_ref[:, 2 * i * dv : 2 * (i + 1) * dv] = att.T.astype(BF16)
        gq_ref[:, 2 * i * dk : 2 * (i + 1) * dk] = gq.T.astype(BF16)
    ggct[pl.ds(row0, hc), :] = jnp.concatenate(rows_c, axis=0)
    ggwt[pl.ds(row0, hc), :] = jnp.concatenate(rows_w, axis=0)
    gk = mm(gss[:win, :], qs[...], 1, 0)
    gv = mm(ws[:win, :], cs[...], 1, 0)

    @pl.when(part == 0)
    def _():
        acck[...] = gk
        accv[...] = gv

    @pl.when(part > 0)
    def _():
        acck[...] += gk
        accv[...] += gv

    @pl.when(part == chunks - 1)
    def _():
        send_ref[0, :, :dk] = acck[:lead, :].astype(BF16)
        send_ref[0, :, off:] = accv[:lead, :].astype(BF16)
        own_ref[0, :, :dk] = acck[lead:, :]
        own_ref[0, :, off:] = accv[lead:, :]
        if off > dk:
            send_ref[0, :, dk:off] = jnp.zeros((lead, off - dk), BF16)
            own_ref[0, :, dk:off] = jnp.zeros((rows, off - dk), F32)
        ggc_ref[...] = ggct[...].T
        ggw_ref[...] = ggwt[...].T


def attend(q, c, prepped, gate_c, gate_w, first, count, groups, reach, nb, off, into):
    kall, kt, vall, vt = prepped
    rows = q.shape[0]
    heads = gate_c.shape[1]
    per = heads // groups
    hc = 8
    chunks = per // hc
    dk, dv, total = kall.shape[2], vall.shape[2], kall.shape[1]
    win = (reach + 1) * rows
    dims = (rows, hc, chunks, dk, dv, nb, off, reach, first)
    col = lambda g, p: (0, (first + g) * chunks + p)
    grp = lambda g, p: (first + g, 0, 0)
    whole = lambda g, p: (0, 0)
    sds = jax.ShapeDtypeStruct
    in_specs = [
        pl.BlockSpec((rows, hc * dk), col),
        pl.BlockSpec((rows, hc * dv), col),
        pl.BlockSpec((1, total, dk), grp),
        pl.BlockSpec((1, dk, total), grp),
        pl.BlockSpec((1, total, dv), grp),
        pl.BlockSpec((1, dv, total), grp),
        pl.BlockSpec((rows, heads), whole),
        pl.BlockSpec((rows, heads), whole),
    ]
    args = [q, c, kall, kt, vall, vt, gate_c, gate_w]
    aliases = {}
    if into is not None:
        in_specs += [pl.BlockSpec(memory_space=pl.ANY)] * 2
        args += list(into)
        aliases = {8: 0, 9: 1}
    flops = 2 * 2 * 3 * rows * per * count * total * (dk + dv)
    return pl.pallas_call(
        functools.partial(main_kernel, dims, into is not None),
        grid=(count, chunks),
        out_shape=(
            sds((rows, heads * dv), BF16),
            sds((rows, heads * dk), BF16),
            sds((count, reach * rows, off + dv), BF16),
            sds((count, rows, off + dv), F32),
            sds((rows, per * count), F32),
            sds((rows, per * count), F32),
        ),
        in_specs=in_specs,
        out_specs=(
            pl.BlockSpec((rows, hc * dv), col),
            pl.BlockSpec((rows, hc * dk), col),
            pl.BlockSpec((1, reach * rows, off + dv), lambda g, p: (g, 0, 0)),
            pl.BlockSpec((1, rows, off + dv), lambda g, p: (g, 0, 0)),
            pl.BlockSpec((rows, per * count), whole),
            pl.BlockSpec((rows, per * count), whole),
        ),
        scratch_shapes=[
            pltpu.VMEM((total, 2 * rows), F32),
            pltpu.VMEM((heads, rows), F32),
            pltpu.VMEM((heads, rows), F32),
            pltpu.VMEM((per * count, rows), F32),
            pltpu.VMEM((per * count, rows), F32),
            pltpu.VMEM((hc * rows, dk), BF16),
            pltpu.VMEM((hc * rows, dv), BF16),
            pltpu.VMEM((total, hc * rows), BF16),
            pltpu.VMEM((total, hc * rows), BF16),
            pltpu.VMEM((win, dk), F32),
            pltpu.VMEM((win, dv), F32),
        ],
        input_output_aliases=aliases,
        cost_estimate=pl.CostEstimate(flops=4 * flops, bytes_accessed=rows * heads * (dk + dv) * 4, transcendentals=0),
        compiler_params=pltpu.CompilerParams(vmem_limit_bytes=VLIM),
    )(*args)


def finish_kernel(dims, cmp_ref, *refs):
    groups, dk, dv, off, halves = dims
    k_ref, v_ref = refs[-2:]
    ins = refs[:-2]
    kw = groups * dk
    each = groups // halves
    per_half = len(ins) // halves
    ks, vs = [], []
    for half in range(halves):
        mine = ins[half * per_half : (half + 1) * per_half]
        for g in range(each):
            total = mine[0][g]
            for ref in mine[1:]:
                total = total + ref[g].astype(F32)
            ks.append(total[:, :dk])
            vs.append(total[:, off:])
    k_ref[...] = (jnp.concatenate(ks, axis=1) + cmp_ref[:, :kw]).astype(BF16)
    v_ref[...] = (jnp.concatenate(vs, axis=1) + cmp_ref[:, kw:]).astype(BF16)


def finish(own_cmp, parts, groups, dk, dv, off, halves):
    rows = own_cmp.shape[0]
    return pl.pallas_call(
        functools.partial(finish_kernel, (groups, dk, dv, off, halves)),
        out_shape=(
            jax.ShapeDtypeStruct((rows, groups * dk), BF16),
            jax.ShapeDtypeStruct((rows, groups * dv), BF16),
        ),
        in_specs=[full()] * (1 + len(parts)),
        out_specs=(full(),) * 2,
        compiler_params=pltpu.CompilerParams(vmem_limit_bytes=VLIM),
    )(own_cmp, *parts)


def send_back(send, rows, reach):
    devices = lax.axis_size("seq")
    got = []
    for distance in range(1, reach + 1):
        at = (reach - distance) * rows
        pairs = [(i, i - distance) for i in range(devices) if i - distance >= 0]
        got.append(lax.ppermute(send[:, at : at + rows], "seq", pairs))
    return got


def on_device(queries, keys_in, values_in, gate_cmp, gate_win, cotangent, compress_key, compress_value):
    rows = queries.shape[1]
    dk, dv = compress_key.shape[1], compress_value.shape[1]
    groups = keys_in.shape[2] // dk
    devices = lax.axis_size("seq")
    reach = (WIN + rows - 1) // rows
    off = up128(dk)
    q, c = queries[0], cotangent[0]
    gc, gw = gate_cmp[0], gate_win[0]
    kv = jnp.concatenate([keys_in[0], values_in[0]], axis=1)
    kv_all = lax.all_gather(kv, "seq", axis=0, tiled=True)
    nb = kv_all.shape[0] // STRIDE
    prepped = prep(kv_all, compress_key, compress_value, groups, rows, reach)
    part = cmp_grads(q, c, prepped[0], prepped[2], gc, groups, reach, nb, off)
    half = groups // 2
    total = lax.psum(part, "seq")
    a = attend(q, c, prepped, gc, gw, 0, half, groups, reach, nb, off, None)
    back_a = send_back(a[2], rows, reach)
    total, att, gq = lax.optimization_barrier((total, a[0], a[1]))
    gwk, gwv, own_cmp = back(total, kv_all, compress_key, compress_value, groups, rows, off, devices)
    gwk_sum, gwv_sum = lax.psum(gwk, "dp"), lax.psum(gwv, "dp")
    att, gq, own_cmp = lax.optimization_barrier((att, gq, own_cmp))
    b = attend(q, c, prepped, gc, gw, half, groups - half, groups, reach, nb, off, (att, gq))
    back_b = send_back(b[2], rows, reach)
    gk, gv = finish(own_cmp, [a[3], *back_a, b[3], *back_b], groups, dk, dv, off, 2)
    return (
        b[0][None],
        b[1][None],
        gk[None],
        gv[None],
        jnp.concatenate([a[4], b[4]], axis=1)[None],
        jnp.concatenate([a[5], b[5]], axis=1)[None],
        gwk_sum.astype(F32),
        gwv_sum.astype(F32),
    )


def solution(mesh):
    tokens = P("dp", "seq", None)
    in_specs = (tokens,) * 6 + (P(), P())
    out_specs = (tokens,) * 6 + (P("seq", None), P("seq", None))
    return jax.shard_map(on_device, mesh=mesh, in_specs=in_specs, out_specs=out_specs, check_vma=False)
```

time: 334 us -> 188 us (0.56)
  matrix products: 78.4 us -> 0 us
  Pallas kernels: 0 us -> 63.5 us
  local copies, waits for them, and re-layouts: 61.7 us -> 14.2 us
  waiting for transfers between devices: 96.5 us -> 72.5 us
  blocking collectives: 19.7 us -> 0 us
  starting transfers between devices: 36.2 us -> 17.3 us
  other arithmetic: 22.7 us -> 4.34 us
    reduce_scatter x4 -> x0, waiting for transfers between devices: 67.1 us -> none  [the longest x1 40.9 us: on_device(): lax.psum_scatter(weight_k.astype(jnp.bfloat16), 'seq', scatter_dimension=...]
    dot_general x17 -> x0, matrix products: 65.9 us -> none  [the longest x2 15.3 us: attend(): jnp.einsum('tgcd,kgd->tgck', grad_out, values_b, preferred_element_type=j...]
    pallas_call x0 -> x6, Pallas kernels: none -> 63.5 us  [the longest x2 37.7 us: attend(): pl.pallas_call(functools.partial(main_kernel, dims, into is not None), gr...]
    all_gather x0 -> x1, waiting for transfers between devices: none -> 25.8 us  [on_device(): kv_all = lax.all_gather(kv, 'seq', axis=0, tiled=True)]
    all_gather x2 -> x0, blocking collectives: 19.7 us -> none  [the longest x1 11.1 us: on_device(): lax.all_gather(comp_v, 'seq', axis=0, tiled=True)]
    psum x1 -> x2, waiting for transfers between devices: 20.5 us -> 39.5 us  [the longest x1 24.3 us: on_device(): total = lax.psum(part, 'seq')]
    slice x27 -> x2, local copies, waits for them, and re-layouts: 21.2 us -> 2.64 us  [send_back(): got.append(lax.ppermute(send[:, at:at + rows], 'seq', pairs))]
    ppermute x16 -> x8, starting transfers between devices: 35.5 us -> 17.2 us  [send_back(): got.append(lax.ppermute(send[:, at:at + rows], 'seq', pairs))]
  transfers between devices with their start and end apart: 21 -> 11, of which waited for: 6 -> 4; matrix products, arithmetic and copies ran while one was open for 35% -> 7% of each run, Pallas kernels for 0% -> 25%
where the time goes in v1:
time: 188 us; the launch traced here: 186 us
  waiting for transfers between devices  72.5 us (39%)
  Pallas kernels  63.5 us (34%)
  starting transfers between devices  17.3 us (9%)
  local copies, waits for them, and re-layouts  14.2 us (8%)
  between operations  14 us (7%)
  other arithmetic  4.34 us (2%)
    pallas_call x2, Pallas kernels, attend(): pl.pallas_call(functools.partial(main_kernel, dims, into is not None), gr...  37.7 us
    all_gather x1, waiting for transfers between devices, on_device(): kv_all = lax.all_gather(kv, 'seq', axis=0, tiled=True)  25.8 us
    psum x1, waiting for transfers between devices, on_device(): total = lax.psum(part, 'seq')  24.3 us
    ppermute x8, starting transfers between devices, send_back(): got.append(lax.ppermute(send[:, at:at + rows], 'seq', pairs))  17.2 us
    psum x1, waiting for transfers between devices, on_device(): gwk_sum, gwv_sum = (lax.psum(gwk, 'dp'), lax.psum(gwv, 'dp'))  15.2 us
    unnamed x26, local copies, waits for them, and re-layouts  11.6 us
    pallas_call x1, Pallas kernels, prep(): pl.pallas_call(functools.partial(prep_kernel, dims), out_shape=(sds(group...  9.74 us
    ppermute x8, waiting for transfers between devices, send_back(): got.append(lax.ppermute(send[:, at:at + rows], 'seq', pairs))  7.11 us
  transfers between devices with their start and end apart: 11, of which 4 were waited for; matrix products, arithmetic and copies ran while one was open for 7% of the time, Pallas kernels for 25%

profile of v1, /device:TPU:3, one launch (start us, length us, event | category | flops | bytes accessed | tf_op | source)
XLA Modules:
  0.0 185.8 jit_solution(9718696049612589420)
XLA Ops:
  7.2 1.7 pad_maximum_fusion
  9.0 1.5 copy.19
  10.5 1.5 copy.20
  12.0 4.5 %copy.18.wk_ref = bf16[6144,192]{1,0:T(8,128)(2,1)} copy(bf16[6144,192]{0,1:T(8,128)(2,1)} %param.14) | data formatting | bytes 4718592 | tf_op args[6]
  16.5 25.8 %all-gather.2.cloned.1.call-done.kv_ref = bf16[1024,1280]{1,0:T(8,128)(2,1)} async-done(((bf16[128,1280]{1,0:T(8,128)(2,1)}), bf16[1024,1280]{1,0:T(8,128)(2,1)}) %all-gather.2.cloned.1.call-update) | async-done | bytes 2621456 | tf_op jit(solution)/shard_map/all_gather | solution.py:445
  42.3 9.7 %shard_map.143 = (bf16[4,704,192]{2,1,0:T(8,128)(2,1)}, bf16[4,192,704]{2,1,0:T(8,128)(2,1)}, bf16[4,704,128]{2,1,0:T(8,128)(2,1)}, bf16[4,128,704]{2,1,0:T(8,128)(2,1)}) custom-call(bf16[1024,1280]{1,0:T(8,128)(2,1)} %all-gather.2.cloned.1.call-done.kv_ref, bf16[6144,192]{1,0:T(8,128)(2,1)} %copy.18.wk_ref, bf16[4096,128]{1,0:T(8,128)(2,1)} %wv_ref.3), custom_call_target="tpu_custom_call" | custom-call | tf_op jit(solution)/shard_map/pallas_call | solution.py:78
  52.0 6.8 %shard_map.144 = bf16[256,384]{1,0:T(8,128)(2,1)} custom-call(bf16[128,12288]{1,0:T(8,128)(2,1)} %bitcast.14, bf16[128,8192]{1,0:T(8,128)(2,1)} %bitcast.17, bf16[4,704,192]{2,1,0:T(8,128)(2,1)} %get-tuple-element.35.k_ref.refs_2_, bf16[4,704,128]{2,1,0:T(8,128)(2,1)} %get-tuple-element.37.v_ref.refs_4_, f32[128,64]{1,0:T(8,128)} %bitcast.20), custom_call_target="tpu_custom_call" | custom-call | tf_op jit(solution)/shard_map/pallas_call | solution.py:225
  58.9 18.9 %shard_map.145 = (bf16[128,8192]{1,0:T(8,128)(2,1)}, bf16[128,12288]{1,0:T(8,128)(2,1)}, bf16[2,512,384]{2,1,0:T(8,128)(2,1)}, f32[2,128,384]{2,1,0:T(8,128)}, f32[128,32]{1,0:T(8,128)}, /*index=5*/f32[128,32]{1,0:T(8,128)}) custom-call(bf16[128,12288]{1,0:T(8,128)(2,1)} %bitcast.15, bf16[128,8192]{1,0:T(8,128)(2,1)} %bitcast.18, ...), custom_call_target="tpu_custom_call" | custom-call | flops 44291850240 | bytes 10485760 | tf_op jit(solution)/shard_map/pallas_call | solution.py:352
  77.7 1.3 fusion.1
  80.4 2.3 %collective-permute-start.2 = (bf16[2,128,384]{2,1,0:T(8,128)(2,1)S(1)}, bf16[2,128,384]{2,1,0:T(8,128)(2,1)S(1)}, u32[]{:S(2)}, u32[]{:S(2)}) collective-permute-start(bf16[2,128,384]{2,1,0:T(8,128)(2,1)S(1)} %get-tuple-element.77), channel_id=1, source_target_pairs={{3,0},{4,1},{5,2},{6,3},{7,4},{11,8},{12,9},{13,10},{14,11},{15,12... | collective-permute-start | bytes 589832 | tf_op jit(solution)/shard_map/ppermute | solution.py:431
  82.7 1.9 %collective-permute-start.1 = (bf16[2,128,384]{2,1,0:T(8,128)(2,1)S(1)}, bf16[2,128,384]{2,1,0:T(8,128)(2,1)S(1)}, u32[]{:S(2)}, u32[]{:S(2)}) collective-permute-start(bf16[2,128,384]{2,1,0:T(8,128)(2,1)S(1)} %get-tuple-element.78), channel_id=1, source_target_pairs={{2,0},{3,1},{4,2},{5,3},{6,4},{7,5},{10,8},{11,9},{12,10},{13,11},... | collective-permute-start | bytes 589832 | tf_op jit(solution)/shard_map/ppermute | solution.py:431
  84.6 2.1 %collective-permute-start = (bf16[2,128,384]{2,1,0:T(8,128)(2,1)S(1)}, bf16[2,128,384]{2,1,0:T(8,128)(2,1)S(1)}, u32[]{:S(2)}, u32[]{:S(2)}) collective-permute-start(bf16[2,128,384]{2,1,0:T(8,128)(2,1)S(1)} %get-tuple-element.79), channel_id=1, source_target_pairs={{1,0},{2,1},{3,2},{4,3},{5,4},{6,5},{7,6},{9,8},{10,9},{11,10},{12... | collective-permute-start | bytes 589832 | tf_op jit(solution)/shard_map/ppermute | solution.py:431
  86.7 24.3 %all-reduce.4.cloned.1.call-done.gc_ref = bf16[256,384]{1,0:T(8,128)(2,1)} async-done(((bf16[256,384]{1,0:T(8,128)(2,1)}), bf16[256,384]{1,0:T(8,128)(2,1)}) %all-reduce.4.cloned.1.call-update) | async-done | bytes 196624 | tf_op jit(solution)/shard_map/psum | solution.py:450
  111.0 6.5 %shard_map.146 = (bf16[768,192]{1,0:T(8,128)(2,1)}, bf16[512,128]{1,0:T(8,128)(2,1)}, f32[128,1280]{1,0:T(8,128)}) custom-call(bf16[256,384]{1,0:T(8,128)(2,1)} %all-reduce.4.cloned.1.call-done.gc_ref, bf16[1024,1280]{1,0:T(8,128)(2,1)} %all-gather.2.cloned.1.call-done.kv_ref, bf16[6144,192]{1,0:T(8,128)(2,1)} %copy.18.wk_ref, bf16[4096,128]{1,0:T(8,128)(2,1)} %wv_ref.3), custom_call_target="tpu_custom_call" | custom-call | tf_op jit(solution)/shard_map/pallas_call | solution.py:135
  117.5 18.9 %shard_map.147 = (bf16[128,8192]{1,0:T(8,128)(2,1)}, bf16[128,12288]{1,0:T(8,128)(2,1)}, bf16[2,512,384]{2,1,0:T(8,128)(2,1)}, f32[2,128,384]{2,1,0:T(8,128)}, f32[128,32]{1,0:T(8,128)}, /*index=5*/f32[128,32]{1,0:T(8,128)}) custom-call(bf16[128,12288]{1,0:T(8,128)(2,1)} %bitcast.16, ...), custom_call_target="tpu_custom_call", output_to_operand_aliasing={{0}: (8, {}), {1}: (9, {})} | custom-call | flops 44291850240 | bytes 10485760 | tf_op jit(solution)/shard_map/pallas_call | solution.py:352
  136.4 1.3 fusion
  139.1 4.4 %collective-permute-start.6 = (bf16[2,128,384]{2,1,0:T(8,128)(2,1)S(1)}, bf16[2,128,384]{2,1,0:T(8,128)(2,1)S(1)}, u32[]{:S(2)}, u32[]{:S(2)}) collective-permute-start(bf16[2,128,384]{2,1,0:T(8,128)(2,1)S(1)} %get-tuple-element.73), channel_id=1, source_target_pairs={{3,0},{4,1},{5,2},{6,3},{7,4},{11,8},{12,9},{13,10},{14,11},{15,12... | collective-permute-start | bytes 589832 | tf_op jit(solution)/shard_map/ppermute | solution.py:431
  143.5 1.9 %collective-permute-start.5 = (bf16[2,128,384]{2,1,0:T(8,128)(2,1)S(1)}, bf16[2,128,384]{2,1,0:T(8,128)(2,1)S(1)}, u32[]{:S(2)}, u32[]{:S(2)}) collective-permute-start(bf16[2,128,384]{2,1,0:T(8,128)(2,1)S(1)} %get-tuple-element.74), channel_id=1, source_target_pairs={{2,0},{3,1},{4,2},{5,3},{6,4},{7,5},{10,8},{11,9},{12,10},{13,11},... | collective-permute-start | bytes 589832 | tf_op jit(solution)/shard_map/ppermute | solution.py:431
  145.4 1.9 %collective-permute-start.4 = (bf16[2,128,384]{2,1,0:T(8,128)(2,1)S(1)}, bf16[2,128,384]{2,1,0:T(8,128)(2,1)S(1)}, u32[]{:S(2)}, u32[]{:S(2)}) collective-permute-start(bf16[2,128,384]{2,1,0:T(8,128)(2,1)S(1)} %get-tuple-element.75), channel_id=1, source_target_pairs={{1,0},{2,1},{3,2},{4,3},{5,4},{6,5},{7,6},{9,8},{10,9},{11,10},{12... | collective-permute-start | bytes 589832 | tf_op jit(solution)/shard_map/ppermute | solution.py:431
  149.8 7.1 %collective-permute-done.6.refs_8_ = bf16[2,128,384]{2,1,0:T(8,128)(2,1)S(1)} collective-permute-done((bf16[2,128,384]{2,1,0:T(8,128)(2,1)S(1)}, bf16[2,128,384]{2,1,0:T(8,128)(2,1)S(1)}, u32[]{:S(2)}, u32[]{:S(2)}) %collective-permute-start.6) | collective-permute-done | bytes 196640 | tf_op jit(solution)/shard_map/ppermute | solution.py:431
  157.7 2.7 %shard_map.148 = (bf16[128,768]{1,0:T(8,128)(2,1)}, bf16[128,512]{1,0:T(8,128)(2,1)}) custom-call(f32[128,1280]{1,0:T(8,128)} %get-tuple-element.49.cmp_ref, f32[2,128,384]{2,1,0:T(8,128)} %get-tuple-element.50.refs_0_, bf16[2,128,384]{2,1,0:T(8,128)(2,1)} %copy-done.3, bf16[2,128,384]{2,1,0:T(8,128)(2,1)} %copy-done.2, bf16[2,128,384]{2,1,0:T(8,128)(2,1)} %copy-done.1, ...), custom_call_target="tpu_custom_call" | custom-call | tf_op jit(solution)/shard_map/pallas_call | solution.py:413
  160.4 15.2 %all-reduce.6.cloned.1.call-done = (bf16[768,192]{1,0:T(8,128)(2,1)}, bf16[512,128]{1,0:T(8,128)(2,1)}) async-done(((bf16[768,192]{1,0:T(8,128)(2,1)}, bf16[512,128]{1,0:T(8,128)(2,1)}), (bf16[768,192]{1,0:T(8,128)(2,1)}, bf16[512,128]{1,0:T(8,128)(2,1)})) %all-reduce.6.cloned.1.call-update) | async-done | bytes 426000 | tf_op jit(solution)/shard_map/psum | solution.py:455
  175.6 2.0 %copy.24 = f32[768,192]{0,1:T(8,128)} copy(bf16[768,192]{1,0:T(8,128)(2,1)} %get-tuple-element.70) | data formatting | bytes 884736
  177.6 1.6 convert_element_type.7
  (38 shorter events, 5.9 us)
Async XLA Ops:
  7.2 35.1 %all-gather.2.cloned.1.call-start = ((), (), s32[]{:S(2)}) async-start(), calls=%async_computation | async-start | bytes 2949120 | tf_op jit(solution)/shard_map/all_gather | solution.py:445
  9.0 102.1 %all-reduce.4.cloned.1.call-start = ((), (), s32[]{:S(2)}) async-start(), calls=%async_computation.1 | async-start | bytes 393216 | tf_op jit(solution)/shard_map/psum | solution.py:450
  58.8 116.8 %all-reduce.6.cloned.1.call-start = ((), (), s32[]{:S(2)}) async-start(), calls=%async_computation.2 | async-start | bytes 1048576 | tf_op jit(solution)/shard_map/psum | solution.py:455
  79.1 60.0 %collective-permute-start.3 = (bf16[2,128,384]{2,1,0:T(8,128)(2,1)S(1)}, bf16[2,128,384]{2,1,0:T(8,128)(2,1)S(1)}, u32[]{:S(2)}, u32[]{:S(2)}) collective-permute-start(bf16[2,128,384]{2,1,0:T(8,128)(2,1)S(1)} %get-tuple-element.76), channel_id=1, source_target_pairs={{4,0},{5,1},{6,2},{7,3},{12,8},{13,9},{14,10},{15,11},{20,16},{21,... | collective-permute-start | bytes 589832 | tf_op jit(solution)/shard_map/ppermute | solution.py:431
  80.4 63.1 %collective-permute-start.2 = (bf16[2,128,384]{2,1,0:T(8,128)(2,1)S(1)}, bf16[2,128,384]{2,1,0:T(8,128)(2,1)S(1)}, u32[]{:S(2)}, u32[]{:S(2)}) collective-permute-start(bf16[2,128,384]{2,1,0:T(8,128)(2,1)S(1)} %get-tuple-element.77), channel_id=1, source_target_pairs={{3,0},{4,1},{5,2},{6,3},{7,4},{11,8},{12,9},{13,10},{14,11},{15,12... | collective-permute-start | bytes 589832 | tf_op jit(solution)/shard_map/ppermute | solution.py:431
  82.7 62.7 %collective-permute-start.1 = (bf16[2,128,384]{2,1,0:T(8,128)(2,1)S(1)}, bf16[2,128,384]{2,1,0:T(8,128)(2,1)S(1)}, u32[]{:S(2)}, u32[]{:S(2)}) collective-permute-start(bf16[2,128,384]{2,1,0:T(8,128)(2,1)S(1)} %get-tuple-element.78), channel_id=1, source_target_pairs={{2,0},{3,1},{4,2},{5,3},{6,4},{7,5},{10,8},{11,9},{12,10},{13,11},... | collective-permute-start | bytes 589832 | tf_op jit(solution)/shard_map/ppermute | solution.py:431
  84.6 65.1 %collective-permute-start = (bf16[2,128,384]{2,1,0:T(8,128)(2,1)S(1)}, bf16[2,128,384]{2,1,0:T(8,128)(2,1)S(1)}, u32[]{:S(2)}, u32[]{:S(2)}) collective-permute-start(bf16[2,128,384]{2,1,0:T(8,128)(2,1)S(1)} %get-tuple-element.79), channel_id=1, source_target_pairs={{1,0},{2,1},{3,2},{4,3},{5,4},{6,5},{7,6},{9,8},{10,9},{11,10},{12... | collective-permute-start | bytes 589832 | tf_op jit(solution)/shard_map/ppermute | solution.py:431
  117.5 29.9 %copy-start.8 = (f32[128,32]{1,0:T(8,128)S(1)}, f32[128,32]{1,0:T(8,128)}, u32[]{:S(2)}) copy-start(f32[128,32]{1,0:T(8,128)} %get-tuple-element.56) | copy-start | bytes 49156
  117.5 29.9 %copy-start.9 = (f32[128,32]{1,0:T(8,128)S(1)}, f32[128,32]{1,0:T(8,128)}, u32[]{:S(2)}) copy-start(f32[128,32]{1,0:T(8,128)} %get-tuple-element.58) | copy-start | bytes 49156
  137.7 12.0 %collective-permute-start.7 = (bf16[2,128,384]{2,1,0:T(8,128)(2,1)S(1)}, bf16[2,128,384]{2,1,0:T(8,128)(2,1)S(1)}, u32[]{:S(2)}, u32[]{:S(2)}) collective-permute-start(bf16[2,128,384]{2,1,0:T(8,128)(2,1)S(1)} %get-tuple-element.72), channel_id=1, source_target_pairs={{4,0},{5,1},{6,2},{7,3},{12,8},{13,9},{14,10},{15,11},{20,16},{21,... | collective-permute-start | bytes 589832 | tf_op jit(solution)/shard_map/ppermute | solution.py:431
  139.0 17.8 %copy-start = (bf16[2,128,384]{2,1,0:T(8,128)(2,1)}, bf16[2,128,384]{2,1,0:T(8,128)(2,1)S(1)}, u32[]{:S(2)}) copy-start(bf16[2,128,384]{2,1,0:T(8,128)(2,1)S(1)} %collective-permute-done.3.refs_4_) | copy-start | bytes 589828
  139.1 17.8 %collective-permute-start.6 = (bf16[2,128,384]{2,1,0:T(8,128)(2,1)S(1)}, bf16[2,128,384]{2,1,0:T(8,128)(2,1)S(1)}, u32[]{:S(2)}, u32[]{:S(2)}) collective-permute-start(bf16[2,128,384]{2,1,0:T(8,128)(2,1)S(1)} %get-tuple-element.73), channel_id=1, source_target_pairs={{3,0},{4,1},{5,2},{6,3},{7,4},{11,8},{12,9},{13,10},{14,11},{15,12... | collective-permute-start | bytes 589832 | tf_op jit(solution)/shard_map/ppermute | solution.py:431
  143.5 13.4 %copy-start.1 = (bf16[2,128,384]{2,1,0:T(8,128)(2,1)}, bf16[2,128,384]{2,1,0:T(8,128)(2,1)S(1)}, u32[]{:S(2)}) copy-start(bf16[2,128,384]{2,1,0:T(8,128)(2,1)S(1)} %collective-permute-done.2.refs_3_) | copy-start | bytes 589828
  143.5 13.4 %collective-permute-start.5 = (bf16[2,128,384]{2,1,0:T(8,128)(2,1)S(1)}, bf16[2,128,384]{2,1,0:T(8,128)(2,1)S(1)}, u32[]{:S(2)}, u32[]{:S(2)}) collective-permute-start(bf16[2,128,384]{2,1,0:T(8,128)(2,1)S(1)} %get-tuple-element.74), channel_id=1, source_target_pairs={{2,0},{3,1},{4,2},{5,3},{6,4},{7,5},{10,8},{11,9},{12,10},{13,11},... | collective-permute-start | bytes 589832 | tf_op jit(solution)/shard_map/ppermute | solution.py:431
  145.4 11.5 %copy-start.2 = (bf16[2,128,384]{2,1,0:T(8,128)(2,1)}, bf16[2,128,384]{2,1,0:T(8,128)(2,1)S(1)}, u32[]{:S(2)}) copy-start(bf16[2,128,384]{2,1,0:T(8,128)(2,1)S(1)} %collective-permute-done.1.refs_2_) | copy-start | bytes 589828
  145.4 11.5 %collective-permute-start.4 = (bf16[2,128,384]{2,1,0:T(8,128)(2,1)S(1)}, bf16[2,128,384]{2,1,0:T(8,128)(2,1)S(1)}, u32[]{:S(2)}, u32[]{:S(2)}) collective-permute-start(bf16[2,128,384]{2,1,0:T(8,128)(2,1)S(1)} %get-tuple-element.75), channel_id=1, source_target_pairs={{1,0},{2,1},{3,2},{4,3},{5,4},{6,5},{7,6},{9,8},{10,9},{11,10},{12... | collective-permute-start | bytes 589832 | tf_op jit(solution)/shard_map/ppermute | solution.py:431
  149.8 7.2 %copy-start.3 = (bf16[2,128,384]{2,1,0:T(8,128)(2,1)}, bf16[2,128,384]{2,1,0:T(8,128)(2,1)S(1)}, u32[]{:S(2)}) copy-start(bf16[2,128,384]{2,1,0:T(8,128)(2,1)S(1)} %collective-permute-done.refs_1_) | copy-start | bytes 589828
  149.8 7.2 %copy-start.4 = (bf16[2,128,384]{2,1,0:T(8,128)(2,1)}, bf16[2,128,384]{2,1,0:T(8,128)(2,1)S(1)}, u32[]{:S(2)}) copy-start(bf16[2,128,384]{2,1,0:T(8,128)(2,1)S(1)} %collective-permute-done.7.refs_9_) | copy-start | bytes 589828
  156.9 0.7 copy-start.5
  156.9 0.7 copy-start.6
  156.9 0.8 copy-start.7
Sparse Core Ops, SparseCore 0:
  10.5 31.7 all-gather.1
  58.9 52.0 all-reduce.3
  136.5 39.0 all-reduce.5

commit v2 on v1

--- a/solution.py
+++ b/solution.py
@@ -148,6 +148,58 @@
         ],
         compiler_params=pltpu.CompilerParams(vmem_limit_bytes=VLIM),
     )(gc, kv_all, wk, wv)
+
+
+def sum_kernel(n, x_ref, out_ref, parts, red, gath, send1, recv1, send2, recv2):
+    me = lax.axis_index("seq")
+    peers = [lax.rem(me + d, n) for d in range(n)]
+    barrier = pltpu.get_barrier_semaphore()
+    for d in range(1, n):
+        pl.semaphore_signal(barrier, inc=1, device_id={"seq": peers[d]}, device_id_type=pl.DeviceIdType.MESH)
+    pl.semaphore_wait(barrier, n - 1)
+
+    def put(src, dst, send, recv, d):
+        copy = pltpu.make_async_remote_copy(
+            src_ref=src,
+            dst_ref=dst,
+            send_sem=send.at[d],
+            recv_sem=recv.at[d],
+            device_id={"seq": peers[d]},
+            device_id_type=pl.DeviceIdType.MESH,
+        )
+        copy.start()
+        return copy
+
+    out = [put(x_ref.at[peers[d]], parts.at[d], send1, recv1, d) for d in range(1, n)]
+    total = x_ref[me].astype(F32)
+    for d in range(1, n):
+        out[d - 1].wait()
+        total = total + parts[d].astype(F32)
+    red[...] = total.astype(BF16)
+    out = [put(red, gath.at[me], send2, recv2, d) for d in range(1, n)]
+    gath[me] = red[...]
+    for copy in out:
+        copy.wait()
+    out_ref[...] = gath[...]
+
+
+def sum_seq(x):
+    n = lax.axis_size("seq")
+    shape = (n, x.shape[0] // n, x.shape[1])
+    out = pl.pallas_call(
+        functools.partial(sum_kernel, n),
+        out_shape=jax.ShapeDtypeStruct(shape, BF16),
+        in_specs=[full()],
+        out_specs=full(),
+        scratch_shapes=[
+            pltpu.VMEM(shape, BF16),
+            pltpu.VMEM(shape[1:], BF16),
+            pltpu.VMEM(shape, BF16),
+            *[pltpu.SemaphoreType.DMA((n,))] * 4,
+        ],
+        compiler_params=pltpu.CompilerParams(collective_id=0, has_side_effects=True, vmem_limit_bytes=VLIM),
+    )(x.reshape(shape))
+    return out.reshape(x.shape)
 
 
 def bias_win(index, rows, reach):
@@ -446,24 +498,24 @@
     nb = kv_all.shape[0] // STRIDE
     prepped = prep(kv_all, compress_key, compress_value, groups, rows, reach)
     part = cmp_grads(q, c, prepped[0], prepped[2], gc, groups, reach, nb, off)
-    half = groups // 2
-    total = lax.psum(part, "seq")
-    a = attend(q, c, prepped, gc, gw, 0, half, groups, reach, nb, off, None)
-    back_a = send_back(a[2], rows, reach)
-    total, att, gq = lax.optimization_barrier((total, a[0], a[1]))
+    total = sum_seq(part)
     gwk, gwv, own_cmp = back(total, kv_all, compress_key, compress_value, groups, rows, off, devices)
+    kall, gwk, gwv = lax.optimization_barrier((prepped[0], gwk, gwv))
     gwk_sum, gwv_sum = lax.psum(gwk, "dp"), lax.psum(gwv, "dp")
-    att, gq, own_cmp = lax.optimization_barrier((att, gq, own_cmp))
-    b = attend(q, c, prepped, gc, gw, half, groups - half, groups, reach, nb, off, (att, gq))
-    back_b = send_back(b[2], rows, reach)
-    gk, gv = finish(own_cmp, [a[3], *back_a, b[3], *back_b], groups, dk, dv, off, 2)
+    prepped = (kall, *prepped[1:])
+    att, gq, send, own, ggc, ggw = attend(
+        q, c, prepped, gc, gw, 0, groups, groups, reach, nb, off, None
+    )
+    send, gwk_sum, gwv_sum = lax.optimization_barrier((send, gwk_sum, gwv_sum))
+    got = send_back(send, rows, reach)
+    gk, gv = finish(own_cmp, [own, *got], groups, dk, dv, off, 1)
     return (
-        b[0][None],
-        b[1][None],
+        att[None],
+        gq[None],
         gk[None],
         gv[None],
-        jnp.concatenate([a[4], b[4]], axis=1)[None],
-        jnp.concatenate([a[5], b[5]], axis=1)[None],
+        ggc[None],
+        ggw[None],
         gwk_sum.astype(F32),
         gwv_sum.astype(F32),
     )

time: 188 us -> 162 us (0.86)
  waiting for transfers between devices: 72.5 us -> 49.1 us
  starting transfers between devices: 17.3 us -> 8.4 us
  Pallas kernels: 63.5 us -> 72 us
    psum x1 -> x0, waiting for transfers between devices: 24.3 us -> none  [on_device(): total = lax.psum(part, 'seq')]
    ppermute x8 -> x4, waiting for transfers between devices: 7.11 us -> 19.8 us  [send_back(): got.append(lax.ppermute(send[:, at:at + rows], 'seq', pairs))]
    psum x1, waiting for transfers between devices: 15.2 us -> 3.49 us  [on_device(): gwk_sum, gwv_sum = (lax.psum(gwk, 'dp'), lax.psum(gwv, 'dp'))]
    pallas_call x0 -> x1, Pallas kernels: none -> 11.1 us  [sum_seq(): pl.pallas_call(functools.partial(sum_kernel, n), out_shape=jax.ShapeDtype...]
    ppermute x8 -> x4, starting transfers between devices: 17.2 us -> 8.32 us  [send_back(): got.append(lax.ppermute(send[:, at:at + rows], 'seq', pairs))]
    pallas_call x2 -> x1, Pallas kernels: 37.7 us -> 35.2 us  [attend(): pl.pallas_call(functools.partial(main_kernel, dims, into is not None), gr...]
    unnamed x26 -> x16, local copies, waits for them, and re-layouts: 11.6 us -> 12.5 us
  transfers between devices with their start and end apart: 11 -> 6, of which waited for: 4 -> 4; matrix products, arithmetic and copies ran while one was open for 7% -> 8% of each run, Pallas kernels for 25% -> 22%
where the time goes in v2:
time: 162 us; the launch traced here: 161 us
  Pallas kernels  72 us (44%)
  waiting for transfers between devices  49.1 us (30%)
  local copies, waits for them, and re-layouts  14.1 us (9%)
  between operations  14.1 us (9%)
  starting transfers between devices  8.4 us (5%)
  other arithmetic  3.36 us (2%)
    pallas_call x1, Pallas kernels, attend(): pl.pallas_call(functools.partial(main_kernel, dims, into is not None), gr...  35.2 us
    all_gather x1, waiting for transfers between devices, on_device(): kv_all = lax.all_gather(kv, 'seq', axis=0, tiled=True)  25.8 us
    ppermute x4, waiting for transfers between devices, send_back(): got.append(lax.ppermute(send[:, at:at + rows], 'seq', pairs))  19.8 us
    unnamed x16, local copies, waits for them, and re-layouts  12.5 us
    pallas_call x1, Pallas kernels, sum_seq(): pl.pallas_call(functools.partial(sum_kernel, n), out_shape=jax.ShapeDtype...  11.1 us
    pallas_call x1, Pallas kernels, prep(): pl.pallas_call(functools.partial(prep_kernel, dims), out_shape=(sds(group...  9.73 us
    ppermute x4, starting transfers between devices, send_back(): got.append(lax.ppermute(send[:, at:at + rows], 'seq', pairs))  8.32 us
    pallas_call x1, Pallas kernels, cmp_grads(): pl.pallas_call(functools.partial(cmp_kernel, dims), grid=(groups,), out_s...  6.81 us
  transfers between devices with their start and end apart: 6, of which 4 were waited for; matrix products, arithmetic and copies ran while one was open for 8% of the time, Pallas kernels for 22%

profile of v2, /device:TPU:3, one launch (start us, length us, event | category | flops | bytes accessed | tf_op | source)
XLA Modules:
  0.0 161.0 jit_solution(8879895147106459834)
XLA Ops:
  7.2 1.7 %pad_maximum_fusion = bf16[128,1280]{1,0:T(8,128)(2,1)} fusion(bf16[128,512]{1,0:T(8,128)(2,1)} %bitcast.23, bf16[128,768]{1,0:T(8,128)(2,1)} %bitcast.22), kind=kLoop, calls=%fused_computation | loop fusion | flops 655360 | bytes 655360 | tf_op jit(solution)/shard_map/concatenate | solution.py:496
  9.0 1.5 copy.17
  10.5 1.5 copy.19
  12.0 4.5 %copy.16.wk_ref = bf16[6144,192]{1,0:T(8,128)(2,1)} copy(bf16[6144,192]{0,1:T(8,128)(2,1)} %param.14) | data formatting | bytes 4718592 | tf_op args[6]
  16.5 25.8 %all-gather.2.cloned.1.call-done.kv_ref = bf16[1024,1280]{1,0:T(8,128)(2,1)} async-done(((bf16[128,1280]{1,0:T(8,128)(2,1)}), bf16[1024,1280]{1,0:T(8,128)(2,1)}) %all-gather.2.cloned.1.call-update) | async-done | bytes 2621456 | tf_op jit(solution)/shard_map/all_gather | solution.py:497
  42.3 9.7 %shard_map.143 = (bf16[4,704,192]{2,1,0:T(8,128)(2,1)}, bf16[4,192,704]{2,1,0:T(8,128)(2,1)}, bf16[4,704,128]{2,1,0:T(8,128)(2,1)}, bf16[4,128,704]{2,1,0:T(8,128)(2,1)}) custom-call(bf16[1024,1280]{1,0:T(8,128)(2,1)} %all-gather.2.cloned.1.call-done.kv_ref, bf16[6144,192]{1,0:T(8,128)(2,1)} %copy.16.wk_ref, bf16[4096,128]{1,0:T(8,128)(2,1)} %wv_ref.3), custom_call_target="tpu_custom_call" | custom-call | tf_op jit(solution)/shard_map/pallas_call | solution.py:78
  52.0 6.8 %shard_map.144 = bf16[256,384]{1,0:T(8,128)(2,1)} custom-call(bf16[128,12288]{1,0:T(8,128)(2,1)} %bitcast.14, bf16[128,8192]{1,0:T(8,128)(2,1)} %bitcast.16, bf16[4,704,192]{2,1,0:T(8,128)(2,1)} %get-tuple-element.33.k_ref.refs_2_, bf16[4,704,128]{2,1,0:T(8,128)(2,1)} %get-tuple-element.30.v_ref.refs_4_, f32[128,64]{1,0:T(8,128)} %bitcast.20), custom_call_target="tpu_custom_call" | custom-call | tf_op jit(solution)/shard_map/pallas_call | solution.py:277
  58.8 11.1 %shard_map.145 = bf16[8,32,384]{2,1,0:T(8,128)(2,1)} custom-call(bf16[8,32,384]{2,1,0:T(8,128)(2,1)} %bitcast.19), custom_call_target="tpu_custom_call" | custom-call | tf_op jit(solution)/shard_map/pallas_call | solution.py:189
  69.9 6.5 %shard_map.146 = (bf16[768,192]{1,0:T(8,128)(2,1)}, bf16[512,128]{1,0:T(8,128)(2,1)}, f32[128,1280]{1,0:T(8,128)}) custom-call(bf16[256,384]{1,0:T(8,128)(2,1)} %bitcast.18, bf16[1024,1280]{1,0:T(8,128)(2,1)} %all-gather.2.cloned.1.call-done.kv_ref, bf16[6144,192]{1,0:T(8,128)(2,1)} %copy.16.wk_ref, bf16[4096,128]{1,0:T(8,128)(2,1)} %wv_ref.3), custom_call_target="tpu_custom_call" | custom-call | tf_op jit(solution)/shard_map/pallas_call | solution.py:135
  76.4 35.2 %shard_map.147 = (bf16[128,8192]{1,0:T(8,128)(2,1)}, bf16[128,12288]{1,0:T(8,128)(2,1)}, bf16[4,512,384]{2,1,0:T(8,128)(2,1)}, f32[4,128,384]{2,1,0:T(8,128)}, f32[128,64]{1,0:T(8,128)}, /*index=5*/f32[128,64]{1,0:T(8,128)}) custom-call(bf16[128,12288]{1,0:T(8,128)(2,1)} %bitcast.15, bf16[128,8192]{1,0:T(8,128)(2,1)} %bitcast.17, ...), custom_call_target="tpu_custom_call" | custom-call | flops 88583700480 | bytes 10485760 | tf_op jit(solution)/shard_map/pallas_call | solution.py:404
  111.6 3.5 %all-reduce.3.cloned.1.call-done = (bf16[768,192]{1,0:T(8,128)(2,1)}, bf16[512,128]{1,0:T(8,128)(2,1)}) async-done(((bf16[768,192]{1,0:T(8,128)(2,1)}, bf16[512,128]{1,0:T(8,128)(2,1)}), (bf16[768,192]{1,0:T(8,128)(2,1)}, bf16[512,128]{1,0:T(8,128)(2,1)})) %all-reduce.3.cloned.1.call-update) | async-done | bytes 426000 | tf_op jit(solution)/shard_map/psum | solution.py:504
  115.1 1.6 fusion
  116.7 1.3 collective-permute-start.3
  118.0 3.2 %collective-permute-start.2 = (bf16[4,128,384]{2,1,0:T(8,128)(2,1)S(1)}, bf16[4,128,384]{2,1,0:T(8,128)(2,1)S(1)}, u32[]{:S(2)}, u32[]{:S(2)}) collective-permute-start(bf16[4,128,384]{2,1,0:T(8,128)(2,1)S(1)} %get-tuple-element.61), channel_id=1, source_target_pairs={{3,0},{4,1},{5,2},{6,3},{7,4},{11,8},{12,9},{13,10},{14,11},{15,12... | collective-permute-start | bytes 1179656 | tf_op jit(solution)/shard_map/ppermute | solution.py:483
  121.2 1.9 %collective-permute-start.1 = (bf16[4,128,384]{2,1,0:T(8,128)(2,1)S(1)}, bf16[4,128,384]{2,1,0:T(8,128)(2,1)S(1)}, u32[]{:S(2)}, u32[]{:S(2)}) collective-permute-start(bf16[4,128,384]{2,1,0:T(8,128)(2,1)S(1)} %get-tuple-element.62), channel_id=1, source_target_pairs={{2,0},{3,1},{4,2},{5,3},{6,4},{7,5},{10,8},{11,9},{12,10},{13,11},... | collective-permute-start | bytes 1179656 | tf_op jit(solution)/shard_map/ppermute | solution.py:483
  123.1 1.9 %collective-permute-start = (bf16[4,128,384]{2,1,0:T(8,128)(2,1)S(1)}, bf16[4,128,384]{2,1,0:T(8,128)(2,1)S(1)}, u32[]{:S(2)}, u32[]{:S(2)}) collective-permute-start(bf16[4,128,384]{2,1,0:T(8,128)(2,1)S(1)} %get-tuple-element.63), channel_id=1, source_target_pairs={{1,0},{2,1},{3,2},{4,3},{5,4},{6,5},{7,6},{9,8},{10,9},{11,10},{12... | collective-permute-start | bytes 1179656 | tf_op jit(solution)/shard_map/ppermute | solution.py:483
  125.0 1.5 copy.20
  126.6 1.5 copy.21
  128.1 1.6 %convert_element_type.7 = f32[512,128]{1,0:T(8,128)} convert(bf16[512,128]{1,0:T(8,128)(2,1)} %get-tuple-element.49) | non-fusion elementwise | flops 65536 | bytes 393216 | tf_op jit(solution)/shard_map/convert_element_type | solution.py:520
  129.7 1.0 copy.22
  130.7 14.2 %collective-permute-done.3.refs_4_ = bf16[4,128,384]{2,1,0:T(8,128)(2,1)S(1)} collective-permute-done((bf16[4,128,384]{2,1,0:T(8,128)(2,1)S(1)}, bf16[4,128,384]{2,1,0:T(8,128)(2,1)S(1)}, u32[]{:S(2)}, u32[]{:S(2)}) %collective-permute-start.3) | collective-permute-done | bytes 393248 | tf_op jit(solution)/shard_map/ppermute | solution.py:483
  144.9 5.6 %collective-permute-done.2.refs_3_ = bf16[4,128,384]{2,1,0:T(8,128)(2,1)S(1)} collective-permute-done((bf16[4,128,384]{2,1,0:T(8,128)(2,1)S(1)}, bf16[4,128,384]{2,1,0:T(8,128)(2,1)S(1)}, u32[]{:S(2)}, u32[]{:S(2)}) %collective-permute-start.2) | collective-permute-done | bytes 393248 | tf_op jit(solution)/shard_map/ppermute | solution.py:483
  150.5 0.7 copy-done.2
  151.5 2.7 %shard_map.148 = (bf16[128,768]{1,0:T(8,128)(2,1)}, bf16[128,512]{1,0:T(8,128)(2,1)}) custom-call(f32[128,1280]{1,0:T(8,128)} %get-tuple-element.38.cmp_ref, f32[4,128,384]{2,1,0:T(8,128)} %get-tuple-element.39.refs_0_, bf16[4,128,384]{2,1,0:T(8,128)(2,1)} %copy-done.4, bf16[4,128,384]{2,1,0:T(8,128)(2,1)} %copy-done.3, bf16[4,128,384]{2,1,0:T(8,128)(2,1)} %copy-done.2, ...), custom_call_target="tpu_custom_call" | custom-call | tf_op jit(solution)/shard_map/pallas_call | solution.py:465
  (15 shorter events, 0.4 us)
Async XLA Ops:
  7.2 35.1 %all-gather.2.cloned.1.call-start = ((), (), s32[]{:S(2)}) async-start(), calls=%async_computation | async-start | bytes 2949120 | tf_op jit(solution)/shard_map/all_gather | solution.py:497
  9.0 106.1 %all-reduce.3.cloned.1.call-start = ((), (), s32[]{:S(2)}) async-start(), calls=%async_computation.1 | async-start | bytes 1048576 | tf_op jit(solution)/shard_map/psum | solution.py:504
  115.1 14.7 %copy-start = (bf16[768,192]{1,0:T(8,128)(2,1)S(1)}, bf16[768,192]{1,0:T(8,128)(2,1)}, u32[]{:S(2)}) copy-start(bf16[768,192]{1,0:T(8,128)(2,1)} %get-tuple-element.48) | copy-start | bytes 884740
  116.7 28.2 %collective-permute-start.3 = (bf16[4,128,384]{2,1,0:T(8,128)(2,1)S(1)}, bf16[4,128,384]{2,1,0:T(8,128)(2,1)S(1)}, u32[]{:S(2)}, u32[]{:S(2)}) collective-permute-start(bf16[4,128,384]{2,1,0:T(8,128)(2,1)S(1)} %get-tuple-element.60), channel_id=1, source_target_pairs={{4,0},{5,1},{6,2},{7,3},{12,8},{13,9},{14,10},{15,11},{20,16},{21,... | collective-permute-start | bytes 1179656 | tf_op jit(solution)/shard_map/ppermute | solution.py:483
  118.0 32.5 %collective-permute-start.2 = (bf16[4,128,384]{2,1,0:T(8,128)(2,1)S(1)}, bf16[4,128,384]{2,1,0:T(8,128)(2,1)S(1)}, u32[]{:S(2)}, u32[]{:S(2)}) collective-permute-start(bf16[4,128,384]{2,1,0:T(8,128)(2,1)S(1)} %get-tuple-element.61), channel_id=1, source_target_pairs={{3,0},{4,1},{5,2},{6,3},{7,4},{11,8},{12,9},{13,10},{14,11},{15,12... | collective-permute-start | bytes 1179656 | tf_op jit(solution)/shard_map/ppermute | solution.py:483
  121.2 29.3 %collective-permute-start.1 = (bf16[4,128,384]{2,1,0:T(8,128)(2,1)S(1)}, bf16[4,128,384]{2,1,0:T(8,128)(2,1)S(1)}, u32[]{:S(2)}, u32[]{:S(2)}) collective-permute-start(bf16[4,128,384]{2,1,0:T(8,128)(2,1)S(1)} %get-tuple-element.62), channel_id=1, source_target_pairs={{2,0},{3,1},{4,2},{5,3},{6,4},{7,5},{10,8},{11,9},{12,10},{13,11},... | collective-permute-start | bytes 1179656 | tf_op jit(solution)/shard_map/ppermute | solution.py:483
  123.1 27.4 %collective-permute-start = (bf16[4,128,384]{2,1,0:T(8,128)(2,1)S(1)}, bf16[4,128,384]{2,1,0:T(8,128)(2,1)S(1)}, u32[]{:S(2)}, u32[]{:S(2)}) collective-permute-start(bf16[4,128,384]{2,1,0:T(8,128)(2,1)S(1)} %get-tuple-element.63), channel_id=1, source_target_pairs={{1,0},{2,1},{3,2},{4,3},{5,4},{6,5},{7,6},{9,8},{10,9},{11,10},{12... | collective-permute-start | bytes 1179656 | tf_op jit(solution)/shard_map/ppermute | solution.py:483
  144.9 5.6 %copy-start.1 = (bf16[4,128,384]{2,1,0:T(8,128)(2,1)}, bf16[4,128,384]{2,1,0:T(8,128)(2,1)S(1)}, u32[]{:S(2)}) copy-start(bf16[4,128,384]{2,1,0:T(8,128)(2,1)S(1)} %collective-permute-done.3.refs_4_) | copy-start | bytes 1179652
  150.5 0.8 copy-start.2
  150.5 0.9 copy-start.3
  150.5 1.0 copy-start.4
Sparse Core Ops, SparseCore 0:
  10.5 31.7 all-gather.1
  76.5 38.4 all-reduce.2

commit v3 on v2

--- a/solution.py
+++ b/solution.py
@@ -200,6 +200,62 @@
         compiler_params=pltpu.CompilerParams(collective_id=0, has_side_effects=True, vmem_limit_bytes=VLIM),
     )(x.reshape(shape))
     return out.reshape(x.shape)
+
+
+def gather_kernel(n, k_ref, v_ref, out_ref, gath, own, send1, recv1, send2, recv2):
+    me = lax.axis_index("seq")
+    sibling = me + 1 - 2 * lax.rem(me, 2)
+    pairs = n // 2
+    kw = k_ref.shape[1]
+    peers = [lax.rem(me + 2 * d, n) for d in range(1, pairs)]
+    origins = [lax.rem(me + n - 2 * d, n) for d in range(1, pairs)]
+    barrier = pltpu.get_barrier_semaphore()
+    for peer in [sibling, *peers]:
+        pl.semaphore_signal(barrier, inc=1, device_id={"seq": peer}, device_id_type=pl.DeviceIdType.MESH)
+    own[:, :kw] = k_ref[...]
+    own[:, kw:] = v_ref[...]
+    pl.semaphore_wait(barrier, pairs)
+
+    def put(src, slot, send, recv, d, peer):
+        copy = pltpu.make_async_remote_copy(
+            src_ref=src,
+            dst_ref=gath.at[slot],
+            send_sem=send.at[d],
+            recv_sem=recv.at[d],
+            device_id={"seq": peer},
+            device_id_type=pl.DeviceIdType.MESH,
+        )
+        copy.start()
+        return copy
+
+    first = [put(own, me, send1, recv1, d, peers[d - 1]) for d in range(1, pairs)]
+    second = [put(own, me, send2, recv2, 0, sibling)]
+    gath[me] = own[...]
+    for d in range(1, pairs):
+        first[d - 1].wait()
+        second.append(put(gath.at[origins[d - 1]], origins[d - 1], send2, recv2, d, sibling))
+    for copy in second:
+        copy.wait()
+    out_ref[...] = gath[...]
+
+
+def gather_seq(k, v):
+    n = lax.axis_size("seq")
+    width = k.shape[1] + v.shape[1]
+    shape = (n, k.shape[0], width)
+    out = pl.pallas_call(
+        functools.partial(gather_kernel, n),
+        out_shape=jax.ShapeDtypeStruct(shape, BF16),
+        in_specs=[full()] * 2,
+        out_specs=full(),
+        scratch_shapes=[
+            pltpu.VMEM(shape, BF16),
+            pltpu.VMEM(shape[1:], BF16),
+            *[pltpu.SemaphoreType.DMA((n // 2,))] * 4,
+        ],
+        compiler_params=pltpu.CompilerParams(collective_id=1, has_side_effects=True, vmem_limit_bytes=VLIM),
+    )(k, v)
+    return out.reshape(n * k.shape[0], width)
 
 
 def bias_win(index, rows, reach):
@@ -493,8 +549,7 @@
     off = up128(dk)
     q, c = queries[0], cotangent[0]
     gc, gw = gate_cmp[0], gate_win[0]
-    kv = jnp.concatenate([keys_in[0], values_in[0]], axis=1)
-    kv_all = lax.all_gather(kv, "seq", axis=0, tiled=True)
+    kv_all = gather_seq(keys_in[0], values_in[0])
     nb = kv_all.shape[0] // STRIDE
     prepped = prep(kv_all, compress_key, compress_value, groups, rows, reach)
     part = cmp_grads(q, c, prepped[0], prepped[2], gc, groups, reach, nb, off)

time: 162 us -> 155 us (0.957)
  waiting for transfers between devices: 49.1 us -> 22.2 us
  Pallas kernels: 72 us -> 94.8 us
  other arithmetic: 3.36 us -> 1.62 us
    all_gather x1 -> x0, waiting for transfers between devices: 25.8 us -> none  [on_device(): kv_all = lax.all_gather(kv, 'seq', axis=0, tiled=True)]
    pallas_call x0 -> x1, Pallas kernels: none -> 22 us  [gather_seq(): pl.pallas_call(functools.partial(gather_kernel, n), out_shape=jax.ShapeDt...]
    concatenate x1 -> x0, other arithmetic: 1.74 us -> none  [on_device(): kv = jnp.concatenate([keys_in[0], values_in[0]], axis=1)]
    unnamed x16 -> x18, local copies, waits for them, and re-layouts: 12.5 us -> 11.8 us
  transfers between devices with their start and end apart: 6 -> 5, of which waited for: 4 -> 3; matrix products, arithmetic and copies ran while one was open for 8% -> 4% of each run, Pallas kernels for 22% -> 23%
where the time goes in v3:
time: 155 us
  Pallas kernels  94.8 us (61%)
  waiting for transfers between devices  22.2 us (14%)
  between operations  14.1 us (9%)
  local copies, waits for them, and re-layouts  13.3 us (9%)
  starting transfers between devices  8.41 us (5%)
  other arithmetic  1.62 us (1%)
    pallas_call x1, Pallas kernels, attend(): pl.pallas_call(functools.partial(main_kernel, dims, into is not None), gr...  35.3 us
    pallas_call x1, Pallas kernels, gather_seq(): pl.pallas_call(functools.partial(gather_kernel, n), out_shape=jax.ShapeDt...  22 us
    ppermute x4, waiting for transfers between devices, send_back(): got.append(lax.ppermute(send[:, at:at + rows], 'seq', pairs))  19.7 us
    unnamed x18, local copies, waits for them, and re-layouts  11.8 us
    pallas_call x1, Pallas kernels, sum_seq(): pl.pallas_call(functools.partial(sum_kernel, n), out_shape=jax.ShapeDtype...  11.7 us
    pallas_call x1, Pallas kernels, prep(): pl.pallas_call(functools.partial(prep_kernel, dims), out_shape=(sds(group...  9.73 us
    ppermute x4, starting transfers between devices, send_back(): got.append(lax.ppermute(send[:, at:at + rows], 'seq', pairs))  8.37 us
    pallas_call x1, Pallas kernels, cmp_grads(): pl.pallas_call(functools.partial(cmp_kernel, dims), grid=(groups,), out_s...  6.8 us
  transfers between devices with their start and end apart: 5, of which 3 were waited for; matrix products, arithmetic and copies ran while one was open for 4% of the time, Pallas kernels for 23%

profile of v3, /device:TPU:3, one launch (start us, length us, event | category | flops | bytes accessed | tf_op | source)
XLA Modules:
  0.0 154.5 jit_solution(3842311568910733654)
XLA Ops:
  7.2 1.5 copy.17
  8.7 4.5 %copy.16.wk_ref = bf16[6144,192]{1,0:T(8,128)(2,1)} copy(bf16[6144,192]{0,1:T(8,128)(2,1)} %param.14) | data formatting | bytes 4718592 | tf_op args[6]
  13.2 22.0 %shard_map.143 = bf16[8,128,1280]{2,1,0:T(8,128)(2,1)} custom-call(bf16[128,768]{1,0:T(8,128)(2,1)} %bitcast.25, bf16[128,512]{1,0:T(8,128)(2,1)} %bitcast.26), custom_call_target="tpu_custom_call" | custom-call | tf_op jit(solution)/shard_map/pallas_call | solution.py:246
  35.2 9.7 %shard_map.144 = (bf16[4,704,192]{2,1,0:T(8,128)(2,1)}, bf16[4,192,704]{2,1,0:T(8,128)(2,1)}, bf16[4,704,128]{2,1,0:T(8,128)(2,1)}, bf16[4,128,704]{2,1,0:T(8,128)(2,1)}) custom-call(bf16[1024,1280]{1,0:T(8,128)(2,1)} %bitcast.15, bf16[6144,192]{1,0:T(8,128)(2,1)} %copy.16.wk_ref, bf16[4096,128]{1,0:T(8,128)(2,1)} %wv_ref.3), custom_call_target="tpu_custom_call" | custom-call | tf_op jit(solution)/shard_map/pallas_call | solution.py:78
  44.9 6.8 %shard_map.145 = bf16[256,384]{1,0:T(8,128)(2,1)} custom-call(bf16[128,12288]{1,0:T(8,128)(2,1)} %bitcast.17, bf16[128,8192]{1,0:T(8,128)(2,1)} %bitcast.19, bf16[4,704,192]{2,1,0:T(8,128)(2,1)} %get-tuple-element.33.k_ref.refs_2_, bf16[4,704,128]{2,1,0:T(8,128)(2,1)} %get-tuple-element.30.v_ref.refs_4_, f32[128,64]{1,0:T(8,128)} %bitcast.23), custom_call_target="tpu_custom_call" | custom-call | tf_op jit(solution)/shard_map/pallas_call | solution.py:333
  51.7 11.7 %shard_map.146 = bf16[8,32,384]{2,1,0:T(8,128)(2,1)} custom-call(bf16[8,32,384]{2,1,0:T(8,128)(2,1)} %bitcast.22), custom_call_target="tpu_custom_call" | custom-call | tf_op jit(solution)/shard_map/pallas_call | solution.py:189
  63.5 6.5 %shard_map.147 = (bf16[768,192]{1,0:T(8,128)(2,1)}, bf16[512,128]{1,0:T(8,128)(2,1)}, f32[128,1280]{1,0:T(8,128)}) custom-call(bf16[256,384]{1,0:T(8,128)(2,1)} %bitcast.21, bf16[1024,1280]{1,0:T(8,128)(2,1)} %bitcast.16, bf16[6144,192]{1,0:T(8,128)(2,1)} %copy.16.wk_ref, bf16[4096,128]{1,0:T(8,128)(2,1)} %wv_ref.3), custom_call_target="tpu_custom_call" | custom-call | tf_op jit(solution)/shard_map/pallas_call | solution.py:135
  70.0 0.7 copy.19
  70.7 35.3 %shard_map.148 = (bf16[128,8192]{1,0:T(8,128)(2,1)}, bf16[128,12288]{1,0:T(8,128)(2,1)}, bf16[4,512,384]{2,1,0:T(8,128)(2,1)}, f32[4,128,384]{2,1,0:T(8,128)}, f32[128,64]{1,0:T(8,128)}, /*index=5*/f32[128,64]{1,0:T(8,128)}) custom-call(bf16[128,12288]{1,0:T(8,128)(2,1)} %bitcast.18, bf16[128,8192]{1,0:T(8,128)(2,1)} %bitcast.20, ...), custom_call_target="tpu_custom_call" | custom-call | flops 88583700480 | bytes 10485760 | tf_op jit(solution)/shard_map/pallas_call | solution.py:460
  106.1 2.5 %all-reduce.3.cloned.1.call-done = (bf16[768,192]{1,0:T(8,128)(2,1)}, bf16[512,128]{1,0:T(8,128)(2,1)}) async-done(((bf16[768,192]{1,0:T(8,128)(2,1)}, bf16[512,128]{1,0:T(8,128)(2,1)}), (bf16[768,192]{1,0:T(8,128)(2,1)}, bf16[512,128]{1,0:T(8,128)(2,1)})) %all-reduce.3.cloned.1.call-update) | async-done | bytes 426000 | tf_op jit(solution)/shard_map/psum | solution.py:559
  108.5 1.6 %fusion = (bf16[4,128,384]{2,1,0:T(8,128)(2,1)S(1)}, bf16[4,128,384]{2,1,0:T(8,128)(2,1)S(1)}, bf16[4,128,384]{2,1,0:T(8,128)(2,1)S(1)}, bf16[4,128,384]{2,1,0:T(8,128)(2,1)S(1)}) fusion(bf16[4,512,384]{2,1,0:T(8,128)(2,1)} %get-tuple-element.43), kind=kLoop, calls=%fused_computation | loop fusion | bytes 3145728 | tf_op jit(solution)/shard_map/slice | solution.py:539
  110.1 1.3 collective-permute-start.3
  111.4 3.2 %collective-permute-start.2 = (bf16[4,128,384]{2,1,0:T(8,128)(2,1)S(1)}, bf16[4,128,384]{2,1,0:T(8,128)(2,1)S(1)}, u32[]{:S(2)}, u32[]{:S(2)}) collective-permute-start(bf16[4,128,384]{2,1,0:T(8,128)(2,1)S(1)} %get-tuple-element.61), channel_id=1, source_target_pairs={{3,0},{4,1},{5,2},{6,3},{7,4},{11,8},{12,9},{13,10},{14,11},{15,12... | collective-permute-start | bytes 1179656 | tf_op jit(solution)/shard_map/ppermute | solution.py:539
  114.7 1.9 %collective-permute-start.1 = (bf16[4,128,384]{2,1,0:T(8,128)(2,1)S(1)}, bf16[4,128,384]{2,1,0:T(8,128)(2,1)S(1)}, u32[]{:S(2)}, u32[]{:S(2)}) collective-permute-start(bf16[4,128,384]{2,1,0:T(8,128)(2,1)S(1)} %get-tuple-element.62), channel_id=1, source_target_pairs={{2,0},{3,1},{4,2},{5,3},{6,4},{7,5},{10,8},{11,9},{12,10},{13,11},... | collective-permute-start | bytes 1179656 | tf_op jit(solution)/shard_map/ppermute | solution.py:539
  116.6 1.9 %collective-permute-start = (bf16[4,128,384]{2,1,0:T(8,128)(2,1)S(1)}, bf16[4,128,384]{2,1,0:T(8,128)(2,1)S(1)}, u32[]{:S(2)}, u32[]{:S(2)}) collective-permute-start(bf16[4,128,384]{2,1,0:T(8,128)(2,1)S(1)} %get-tuple-element.63), channel_id=1, source_target_pairs={{1,0},{2,1},{3,2},{4,3},{5,4},{6,5},{7,6},{9,8},{10,9},{11,10},{12... | collective-permute-start | bytes 1179656 | tf_op jit(solution)/shard_map/ppermute | solution.py:539
  118.6 1.5 copy.20
  120.1 1.5 copy.21
  121.6 1.6 %convert_element_type.7 = f32[512,128]{1,0:T(8,128)} convert(bf16[512,128]{1,0:T(8,128)(2,1)} %get-tuple-element.49) | non-fusion elementwise | flops 65536 | bytes 393216 | tf_op jit(solution)/shard_map/convert_element_type | solution.py:575
  123.3 1.0 copy.22
  124.2 14.1 %collective-permute-done.3.refs_4_ = bf16[4,128,384]{2,1,0:T(8,128)(2,1)S(1)} collective-permute-done((bf16[4,128,384]{2,1,0:T(8,128)(2,1)S(1)}, bf16[4,128,384]{2,1,0:T(8,128)(2,1)S(1)}, u32[]{:S(2)}, u32[]{:S(2)}) %collective-permute-start.3) | collective-permute-done | bytes 393248 | tf_op jit(solution)/shard_map/ppermute | solution.py:539
  138.3 5.6 %collective-permute-done.2.refs_3_ = bf16[4,128,384]{2,1,0:T(8,128)(2,1)S(1)} collective-permute-done((bf16[4,128,384]{2,1,0:T(8,128)(2,1)S(1)}, bf16[4,128,384]{2,1,0:T(8,128)(2,1)S(1)}, u32[]{:S(2)}, u32[]{:S(2)}) %collective-permute-start.2) | collective-permute-done | bytes 393248 | tf_op jit(solution)/shard_map/ppermute | solution.py:539
  144.0 0.7 copy-done.2
  144.7 0.1 copy-done.3
  145.0 2.7 %shard_map.149 = (bf16[128,768]{1,0:T(8,128)(2,1)}, bf16[128,512]{1,0:T(8,128)(2,1)}) custom-call(f32[128,1280]{1,0:T(8,128)} %get-tuple-element.38.cmp_ref, f32[4,128,384]{2,1,0:T(8,128)} %get-tuple-element.39.refs_0_, bf16[4,128,384]{2,1,0:T(8,128)(2,1)} %copy-done.4, bf16[4,128,384]{2,1,0:T(8,128)(2,1)} %copy-done.3, bf16[4,128,384]{2,1,0:T(8,128)(2,1)} %copy-done.2, ...), custom_call_target="tpu_custom_call" | custom-call | tf_op jit(solution)/shard_map/pallas_call | solution.py:521
  (14 shorter events, 0.2 us)
Async XLA Ops:
  7.2 101.4 %all-reduce.3.cloned.1.call-start = ((), (), s32[]{:S(2)}) async-start(), calls=%async_computation | async-start | bytes 1048576 | tf_op jit(solution)/shard_map/psum | solution.py:559
  63.5 6.5 %copy-start.5 = (f32[1,128,64]{1,2,0:T(8,128)S(1)}, f32[1,128,64]{1,2,0:T(8,128)}, u32[]{:S(2)}) copy-start(f32[1,128,64]{1,2,0:T(8,128)} %param.12) | copy-start | bytes 98308
  108.5 14.7 %copy-start = (bf16[768,192]{1,0:T(8,128)(2,1)S(1)}, bf16[768,192]{1,0:T(8,128)(2,1)}, u32[]{:S(2)}) copy-start(bf16[768,192]{1,0:T(8,128)(2,1)} %get-tuple-element.48) | copy-start | bytes 884740
  110.1 28.2 %collective-permute-start.3 = (bf16[4,128,384]{2,1,0:T(8,128)(2,1)S(1)}, bf16[4,128,384]{2,1,0:T(8,128)(2,1)S(1)}, u32[]{:S(2)}, u32[]{:S(2)}) collective-permute-start(bf16[4,128,384]{2,1,0:T(8,128)(2,1)S(1)} %get-tuple-element.60), channel_id=1, source_target_pairs={{4,0},{5,1},{6,2},{7,3},{12,8},{13,9},{14,10},{15,11},{20,16},{21,... | collective-permute-start | bytes 1179656 | tf_op jit(solution)/shard_map/ppermute | solution.py:539
  111.4 32.5 %collective-permute-start.2 = (bf16[4,128,384]{2,1,0:T(8,128)(2,1)S(1)}, bf16[4,128,384]{2,1,0:T(8,128)(2,1)S(1)}, u32[]{:S(2)}, u32[]{:S(2)}) collective-permute-start(bf16[4,128,384]{2,1,0:T(8,128)(2,1)S(1)} %get-tuple-element.61), channel_id=1, source_target_pairs={{3,0},{4,1},{5,2},{6,3},{7,4},{11,8},{12,9},{13,10},{14,11},{15,12... | collective-permute-start | bytes 1179656 | tf_op jit(solution)/shard_map/ppermute | solution.py:539
  114.7 29.3 %collective-permute-start.1 = (bf16[4,128,384]{2,1,0:T(8,128)(2,1)S(1)}, bf16[4,128,384]{2,1,0:T(8,128)(2,1)S(1)}, u32[]{:S(2)}, u32[]{:S(2)}) collective-permute-start(bf16[4,128,384]{2,1,0:T(8,128)(2,1)S(1)} %get-tuple-element.62), channel_id=1, source_target_pairs={{2,0},{3,1},{4,2},{5,3},{6,4},{7,5},{10,8},{11,9},{12,10},{13,11},... | collective-permute-start | bytes 1179656 | tf_op jit(solution)/shard_map/ppermute | solution.py:539
  116.6 27.3 %collective-permute-start = (bf16[4,128,384]{2,1,0:T(8,128)(2,1)S(1)}, bf16[4,128,384]{2,1,0:T(8,128)(2,1)S(1)}, u32[]{:S(2)}, u32[]{:S(2)}) collective-permute-start(bf16[4,128,384]{2,1,0:T(8,128)(2,1)S(1)} %get-tuple-element.63), channel_id=1, source_target_pairs={{1,0},{2,1},{3,2},{4,3},{5,4},{6,5},{7,6},{9,8},{10,9},{11,10},{12... | collective-permute-start | bytes 1179656 | tf_op jit(solution)/shard_map/ppermute | solution.py:539
  138.3 5.6 %copy-start.1 = (bf16[4,128,384]{2,1,0:T(8,128)(2,1)}, bf16[4,128,384]{2,1,0:T(8,128)(2,1)S(1)}, u32[]{:S(2)}) copy-start(bf16[4,128,384]{2,1,0:T(8,128)(2,1)S(1)} %collective-permute-done.3.refs_4_) | copy-start | bytes 1179652
  143.9 0.8 copy-start.2
  144.0 0.9 copy-start.3
  144.0 1.0 copy-start.4
Sparse Core Ops, SparseCore 0:
  70.1 38.3 all-reduce.2
